TPU v7x, 768 devices: a whole 4x8x12 slice. The times are simulated.
768 devices in a mesh: wide: 192 (over x, y_hi, z), narrow: 4 (over y_lo, core).
Axes of the slice: x: 4, y: 8 (y_hi: 4, y_lo: 2; y = y_hi * 2 + y_lo), z: 12, core: 2. Of those that a mesh axis runs over, the one named last changes fastest.
Arguments:
- image_embeds: bfloat16 [3072, 1152], P(('wide', 'narrow')), may hold values from -16 to 16
- text_embeds: bfloat16 [3072, 1152], P(('wide', 'narrow')), may hold values from -16 to 16
- log_scale: float32 [1], replicated, may hold values from 1.5 to 2.5
- bias: float32 [1], replicated, may hold values from -2 to 0
Outputs:
- row_loss: float32 [3072], P(('wide', 'narrow'))
- image_grad: float32 [3072, 1152], P(('wide', 'narrow'))
- text_grad: float32 [3072, 1152], P(('wide', 'narrow'))
All inputs are finite; a program needn't handle non-finite values.
Results may differ from a plain program's by a relative error of at most 0.0014.
Values may be sent and summed in bfloat16 or wider, within the bound.
No kernel may reach another device: no remote copies, remote signals or barrier semaphores. Data moves between devices by JAX's collectives and lax.ppermute only.
A program may use at most 32 MiB of HBM per device.

v0:
```python
import jax
import jax.numpy as jnp
from jax import lax
from jax.sharding import PartitionSpec as P

epsilon = 1e-06


def unit_rows(embeds):
    values = embeds.astype(jnp.float32)
    inverse = lax.rsqrt(jnp.sum(values * values, axis=1, keepdims=True) + epsilon)
    unit = values * inverse
    return (inverse, unit, unit.astype(jnp.bfloat16))


def backward_unit(inverse, unit, upstream):
    return inverse * (upstream - unit * jnp.sum(unit * upstream, axis=1, keepdims=True))


def pair_terms(image_rows, text_rows, positive, scale_value, bias_value):
    raw_logits = lax.dot_general(
        image_rows, text_rows, (((1,), (1,)), ((), ())), preferred_element_type=jnp.float32
    )
    logits = scale_value * raw_logits + bias_value
    labels = jnp.where(positive, 1.0, -1.0).astype(jnp.float32)
    losses = jnp.sum(jax.nn.softplus(-labels * logits), axis=1)
    coefs = (-scale_value * labels * jax.nn.sigmoid(-labels * logits)).astype(jnp.bfloat16)
    return (losses, coefs)


def project_back(coefs, image_rows):
    return lax.dot_general(
        coefs, image_rows, (((0,), (0,)), ((), ())), preferred_element_type=jnp.float32
    )


def image_side(gathered, every_text, text_count, wide_index, narrow_index, scale_value, bias_value):
    row_ids = jnp.arange(gathered.shape[0], dtype=jnp.int32)[:, None]
    column_ids = jnp.arange(every_text.shape[0], dtype=jnp.int32)[None, :]
    positive = (column_ids // text_count == wide_index) & (
        row_ids == narrow_index * text_count + column_ids % text_count
    )
    loss_sum, coefs = pair_terms(gathered, every_text, positive, scale_value, bias_value)
    image_sum = jnp.dot(coefs, every_text, preferred_element_type=jnp.float32)
    return (loss_sum, coefs, image_sum)


def on_device(image_embeds, text_embeds, log_scale, bias):
    image_inverse, image_unit, image_low = unit_rows(image_embeds)
    text_inverse, text_unit, text_low = unit_rows(text_embeds)
    scale_value = jnp.exp(log_scale[0])
    bias_value = bias[0]
    gathered = lax.all_gather(image_low, "narrow", axis=0, tiled=True)
    text_count = text_low.shape[0]
    wide_count = lax.axis_size("wide")
    narrow_count = lax.axis_size("narrow")
    batch = text_count * wide_count * narrow_count
    narrow_index = lax.axis_index("narrow")
    wide_index = lax.axis_index("wide")
    every_text = lax.all_gather(text_low, "wide", axis=0, tiled=True)
    loss_sum, coefs, image_sum = image_side(
        gathered, every_text, text_count, wide_index, narrow_index, scale_value, bias_value
    )
    text_sum = lax.psum_scatter(
        project_back(coefs, gathered), "wide", scatter_dimension=0, tiled=True
    )
    image_total, loss_total = (
        lax.psum_scatter(image_sum, "narrow", scatter_dimension=0, tiled=True),
        lax.psum_scatter(loss_sum, "narrow", scatter_dimension=0, tiled=True),
    )
    row_loss = loss_total / batch
    image_grad = backward_unit(image_inverse, image_unit, image_total)
    text_grad = backward_unit(text_inverse, text_unit, text_sum)
    return (row_loss, image_grad, text_grad)


def solution(mesh):
    in_specs = (P(("wide", "narrow"), None), P(("wide", "narrow"), None), P(), P())
    out_specs = (P(("wide", "narrow")), P(("wide", "narrow"), None), P(("wide", "narrow"), None))
    return jax.shard_map(
        on_device, mesh=mesh, in_specs=in_specs, out_specs=out_specs, check_vma=False
    )
```

profile of v0, /device:TPU:64, one launch (start us, length us, event | category | flops | bytes accessed | tf_op | source)
XLA Modules:
  0.0 2347.9 jit_solution(15696995710967964505)
XLA Ops:
  7.2 0.0 all-gather.4.cloned.1.call-start
  7.2 0.8 fusion.19
  8.0 1.4 fusion.21
  9.4 0.0 all-gather.4.cloned.1.call-update
  9.4 0.0 all-reduce.6.cloned.1.call-start
  10.8 0.8 fusion.15
  11.7 0.8 fusion.20
  12.4 5.2 all-gather
  17.7 165.4 %all-gather.4.cloned.1.call-done = bf16[192,4,1152]{2,1,0:T(4,128)(2,1)} async-done(((bf16[1,4,1152]{2,1,0:T(4,128)(2,1)}), bf16[192,4,1152]{2,1,0:T(4,128)(2,1)}) %all-gather.4.cloned.1.call-update) | async-done | bytes 1769488 | tf_op jit(solution)/shard_map/all_gather | solution.py:60
  183.1 2.9 reshape.80
  186.0 0.7 fusion.4
  186.7 1.0 fusion.33
  187.7 0.0 all-reduce.6.cloned.1.call-update
  187.7 0.0 all-reduce.8.cloned.1.call-start
  187.8 2.5 fusion.31
  190.3 0.0 copy-start
  190.3 0.0 copy-start.1
  190.3 0.0 all-reduce.8.cloned.1.call-update
  190.3 1.3 dynamic-slice.4
  191.6 1.3 dynamic-slice
  194.1 6.0 all-reduce
  200.1 0.6 dynamic-slice_multiply_fusion
  200.7 34.1 %all-reduce.6.cloned.1.call-done = f32[16,1152]{1,0:T(8,128)} async-done(((f32[16,1152]{1,0:T(8,128)}), f32[16,1152]{1,0:T(8,128)}) %all-reduce.6.cloned.1.call-update) | async-done | bytes 73744
  234.8 0.0 copy-done
  234.8 1.0 fusion.12
  235.8 1.5 fusion.14
  237.2 2101.7 %all-reduce.8.cloned.1.call-done = f32[768,1152]{1,0:T(8,128)} async-done(((f32[768,1152]{1,0:T(8,128)}), f32[768,1152]{1,0:T(8,128)}) %all-reduce.8.cloned.1.call-update) | async-done | bytes 3538960
  2338.9 0.0 copy-done.1
  2338.9 1.0 fusion.16
  2339.9 1.5 fusion.18
  (5 shorter events, 0.0 us)
Async XLA Ops:
  7.2 175.9 %all-gather.4.cloned.1.call-start = ((), (), s32[]{:S(2)}) async-start(), calls=%async_computation | async-start | bytes 1778688 | tf_op jit(solution)/shard_map/all_gather | solution.py:60
  9.4 225.4 %all-reduce.6.cloned.1.call-start = ((), (), s32[]{:S(2)}) async-start(), calls=%async_computation.1 | async-start | bytes 147456
  187.7 2151.2 %all-reduce.8.cloned.1.call-start = ((), (), s32[]{:S(2)}) async-start(), calls=%async_computation.2 | async-start | bytes 7077888
  190.3 44.6 %copy-start = (bf16[4,1152]{1,0:T(4,128)(2,1)S(1)}, bf16[4,1152]{1,0:T(4,128)(2,1)}, u32[]{:S(2)}) copy-start(bf16[4,1152]{1,0:T(4,128)(2,1)} %param.4) | copy-start | bytes 27652
  190.3 2148.7 %copy-start.1 = (bf16[4,1152]{1,0:T(4,128)(2,1)S(1)}, bf16[4,1152]{1,0:T(4,128)(2,1)}, u32[]{:S(2)}) copy-start(bf16[4,1152]{1,0:T(4,128)(2,1)} %param.5) | copy-start | bytes 27652
Sparse Core Ops, SparseCore 0:
  13.8 169.2 all-gather.3
  187.8 46.9 all-reduce.5
  238.4 2100.4 all-reduce.7
where the time goes:
time: 2350 us
  waiting for transfers between devices  2300 us (98%)
    unnamed x5, waiting for transfers between devices  2140 us
    all_gather x1, waiting for transfers between devices, on_device(): every_text = lax.all_gather(text_low, 'wide', axis=0, tiled=True)  165 us
  transfers between devices with their start and end apart: 3, of which 3 were waited for; matrix products, arithmetic and copies ran while one was open for 0% of the time, Pallas kernels for 0%

commit v1 on v0

v1 whole, which is shorter than its diff:
```python
import jax
import jax.numpy as jnp
from jax import lax
from jax.sharding import Mesh
from jax.sharding import PartitionSpec as P

epsilon = 1e-06
AXES = ("x", "yh", "z", "yl", "c")
SIZES = (4, 4, 12, 2, 2)
IMAGE = ("z", "c")
TEXT = ("x", "yh", "yl")


def unit_rows(embeds):
    values = embeds.astype(jnp.float32)
    inverse = lax.rsqrt(jnp.sum(values * values, axis=1, keepdims=True) + epsilon)
    unit = values * inverse
    return (inverse, unit, unit.astype(jnp.bfloat16))


def backward_unit(inverse, unit, upstream):
    return inverse * (upstream - unit * jnp.sum(unit * upstream, axis=1, keepdims=True))


def share_rows(rows, axes):
    count = lax.axis_size(axes)
    copies = jnp.broadcast_to(rows[None], (count,) + rows.shape)
    return lax.all_to_all(copies, axes, 0, 0, tiled=True).reshape(count * rows.shape[0], -1)


def sum_rows(parts, axes):
    count = lax.axis_size(axes)
    pieces = parts.reshape(count, parts.shape[0] // count, parts.shape[1])
    return jnp.sum(lax.all_to_all(pieces, axes, 0, 0, tiled=True), axis=0)


def on_device(image_embeds, text_embeds, log_scale, bias):
    rows, width = image_embeds.shape
    batch = rows * lax.axis_size(AXES)
    image_inverse, image_unit, image_low = unit_rows(image_embeds)
    text_inverse, text_unit, text_low = unit_rows(text_embeds)
    scale_value = jnp.exp(log_scale[0])
    bias_value = bias[0]
    images = share_rows(image_low, IMAGE)
    texts = share_rows(text_low, TEXT)
    row_ids = jnp.arange(images.shape[0], dtype=jnp.int32)[:, None] - rows * lax.axis_index(IMAGE)
    column_ids = jnp.arange(texts.shape[0], dtype=jnp.int32)[None, :] - rows * lax.axis_index(TEXT)
    positive = (row_ids == column_ids) & (row_ids >= 0) & (row_ids < rows)
    raw_logits = lax.dot_general(
        images, texts, (((1,), (1,)), ((), ())), preferred_element_type=jnp.float32
    )
    logits = scale_value * raw_logits + bias_value
    labels = jnp.where(positive, 1.0, -1.0).astype(jnp.float32)
    losses = jnp.sum(jax.nn.softplus(-labels * logits), axis=1, keepdims=True)
    coefs = (-scale_value * labels * jax.nn.sigmoid(-labels * logits)).astype(jnp.bfloat16)
    image_part = jnp.dot(coefs, texts, preferred_element_type=jnp.float32)
    text_part = lax.dot_general(
        coefs, images, (((0,), (0,)), ((), ())), preferred_element_type=jnp.float32
    )
    packed = jnp.concatenate([image_part, jnp.broadcast_to(losses, (losses.shape[0], 128))], axis=1)
    image_sum = sum_rows(packed, IMAGE)
    text_sum = sum_rows(text_part, TEXT)
    row_loss = image_sum[:, width] / batch
    image_grad = backward_unit(image_inverse, image_unit, image_sum[:, :width])
    text_grad = backward_unit(text_inverse, text_unit, text_sum)
    return (row_loss, image_grad, text_grad)


def solution(mesh):
    fine = Mesh(mesh.devices.reshape(SIZES), AXES)
    in_specs = (P(AXES, None), P(AXES, None), P(), P())
    out_specs = (P(AXES), P(AXES, None), P(AXES, None))
    return jax.shard_map(
        on_device, mesh=fine, in_specs=in_specs, out_specs=out_specs, check_vma=False
    )
```

time: 2350 us -> 112 us (0.05)
  the two profiles are of different devices: /device:TPU:64 before, /device:TPU:1 now
where the time goes in v1:
time: 112 us; the launch traced here: 110 us
  waiting for transfers between devices  56.6 us (51%)
  starting transfers between devices  42.7 us (38%)
  local copies, waits for them, and re-layouts  4.01 us (4%)
  other arithmetic  3.94 us (4%)
  between operations  2.13 us (2%)
    all_to_all x2, waiting for transfers between devices, sum_rows(): return jnp.sum(lax.all_to_all(pieces, axes, 0, 0, tiled=True), axis=0)  34.2 us
    all_to_all x2, starting transfers between devices, share_rows(): lax.all_to_all(copies, axes, 0, 0, tiled=True)  29.8 us
    all_to_all x2, waiting for transfers between devices, share_rows(): lax.all_to_all(copies, axes, 0, 0, tiled=True)  22.5 us
    all_to_all x2, starting transfers between devices, sum_rows(): return jnp.sum(lax.all_to_all(pieces, axes, 0, 0, tiled=True), axis=0)  12.9 us
  transfers between devices with their start and end apart: 4, of which 4 were waited for; matrix products, arithmetic and copies ran while one was open for 2% of the time, Pallas kernels for 0%

profile of v1, /device:TPU:1, one launch (start us, length us, event | category | flops | bytes accessed | tf_op | source)
XLA Modules:
  0.0 110.3 jit_solution(3054668127501629770)
XLA Ops:
  0.6 0.9 fusion.36
  1.5 0.1 fusion.25
  1.6 0.8 broadcast_in_dim.21
  2.4 10.6 %all-to-all-start.1 = ((bf16[32,4,1152]{2,1,0:T(4,128)(2,1)}), bf16[32,4,1152]{2,1,0:T(4,128)(2,1)S(1)}, u32[]{:S(2)}, u32[]{:S(2)}) async-start(bf16[32,4,1152]{2,1,0:T(4,128)(2,1)} %broadcast_in_dim.21), calls=%async_computation.1 | async-start | bytes 589824 | tf_op jit(solution)/shard_map/all_to_all | solution.py:28
  13.1 0.1 fusion.32
  13.2 0.1 fusion.28
  13.3 9.6 %all-to-all-done.1 = bf16[32,4,1152]{2,1,0:T(4,128)(2,1)S(1)} async-done(((bf16[32,4,1152]{2,1,0:T(4,128)(2,1)}), bf16[32,4,1152]{2,1,0:T(4,128)(2,1)S(1)}, u32[]{:S(2)}, u32[]{:S(2)}) %all-to-all-start.1) | async-done | bytes 294944 | tf_op jit(solution)/shard_map/all_to_all | solution.py:28
  22.9 0.7 broadcast_in_dim.20
  23.6 19.2 %all-to-all-start = ((bf16[24,4,1152]{2,1,0:T(4,128)(2,1)}), bf16[24,4,1152]{2,1,0:T(4,128)(2,1)S(1)}, u32[]{:S(2)}, u32[]{:S(2)}) async-start(bf16[24,4,1152]{2,1,0:T(4,128)(2,1)} %broadcast_in_dim.20), calls=%async_computation | async-start | bytes 442368 | tf_op jit(solution)/shard_map/all_to_all | solution.py:28
  44.2 0.1 reshape.54
  44.3 12.8 %all-to-all-done = bf16[24,4,1152]{2,1,0:T(4,128)(2,1)S(1)} async-done(((bf16[24,4,1152]{2,1,0:T(4,128)(2,1)}), bf16[24,4,1152]{2,1,0:T(4,128)(2,1)S(1)}, u32[]{:S(2)}, u32[]{:S(2)}) %all-to-all-start) | async-done | bytes 221216 | tf_op jit(solution)/shard_map/all_to_all | solution.py:28
  57.2 0.1 reshape.53
  57.2 0.4 fusion.11
  57.6 0.1 fusion.5
  57.7 0.1 copy.10
  57.8 0.1 reshape.56
  57.9 0.2 fusion.12
  58.1 1.2 %copy.12 = f32[32,4,1152]{2,1,0:T(4,128)} copy(f32[32,4,1152]{2,0,1:T(8,128)S(1)} %fusion.12) | data formatting | bytes 1179648 | tf_op jit(solution)/shard_map/dot_general | solution.py:57
  59.3 4.4 %all-to-all-start.3 = ((f32[32,4,1152]{2,1,0:T(4,128)}), f32[32,4,1152]{2,1,0:T(4,128)S(1)}, u32[]{:S(2)}, u32[]{:S(2)}) async-start(f32[32,4,1152]{2,1,0:T(4,128)} %copy.12), calls=%async_computation.3 | async-start | bytes 1179648 | tf_op jit(solution)/shard_map/all_to_all | solution.py:34
  63.7 0.3 fusion.14
  64.0 0.1 broadcast_in_dim.40
  64.1 0.9 reshape.55
  65.0 13.7 %all-to-all-done.3 = f32[32,4,1152]{2,1,0:T(4,128)S(1)} async-done(((f32[32,4,1152]{2,1,0:T(4,128)}), f32[32,4,1152]{2,1,0:T(4,128)S(1)}, u32[]{:S(2)}, u32[]{:S(2)}) %all-to-all-start.3) | async-done | bytes 589856 | tf_op jit(solution)/shard_map/all_to_all | solution.py:34
  78.7 8.5 %all-to-all-start.2 = ((f32[24,4,1280]{2,1,0:T(4,128)}), f32[24,4,1280]{2,1,0:T(4,128)S(1)}, u32[]{:S(2)}, u32[]{:S(2)}) async-start(f32[24,4,1280]{2,1,0:T(4,128)} %reshape.55), calls=%async_computation.2 | async-start | bytes 983040 | tf_op jit(solution)/shard_map/all_to_all | solution.py:34
  87.3 0.1 reduce_sum.68
  87.4 0.2 fusion.33
  87.6 0.7 fusion.35
  88.2 20.5 %all-to-all-done.2 = f32[24,4,1280]{2,1,0:T(4,128)S(1)} async-done(((f32[24,4,1280]{2,1,0:T(4,128)}), f32[24,4,1280]{2,1,0:T(4,128)S(1)}, u32[]{:S(2)}, u32[]{:S(2)}) %all-to-all-start.2) | async-done | bytes 491552 | tf_op jit(solution)/shard_map/all_to_all | solution.py:34
  108.7 0.1 reduce_sum.66
  108.8 0.2 fusion.29
  109.0 0.6 fusion.37
  109.6 0.7 fusion.31
  (10 shorter events, 0.1 us)
Async XLA Ops:
  0.6 0.9 copy-start
  2.4 10.6 %copy-start.1 = (bf16[4,1152]{1,0:T(4,128)(2,1)S(1)}, bf16[4,1152]{1,0:T(4,128)(2,1)}, u32[]{:S(2)}) copy-start(bf16[4,1152]{1,0:T(4,128)(2,1)} %param.4) | copy-start | bytes 27652
  2.4 20.5 %all-to-all-start.1 = ((bf16[32,4,1152]{2,1,0:T(4,128)(2,1)}), bf16[32,4,1152]{2,1,0:T(4,128)(2,1)S(1)}, u32[]{:S(2)}, u32[]{:S(2)}) async-start(bf16[32,4,1152]{2,1,0:T(4,128)(2,1)} %broadcast_in_dim.21), calls=%async_computation.1 | async-start | bytes 589824 | tf_op jit(solution)/shard_map/all_to_all | solution.py:28
  23.6 33.5 %all-to-all-start = ((bf16[24,4,1152]{2,1,0:T(4,128)(2,1)}), bf16[24,4,1152]{2,1,0:T(4,128)(2,1)S(1)}, u32[]{:S(2)}, u32[]{:S(2)}) async-start(bf16[24,4,1152]{2,1,0:T(4,128)(2,1)} %broadcast_in_dim.20), calls=%async_computation | async-start | bytes 442368 | tf_op jit(solution)/shard_map/all_to_all | solution.py:28
  59.3 19.4 %all-to-all-start.3 = ((f32[32,4,1152]{2,1,0:T(4,128)}), f32[32,4,1152]{2,1,0:T(4,128)S(1)}, u32[]{:S(2)}, u32[]{:S(2)}) async-start(f32[32,4,1152]{2,1,0:T(4,128)} %copy.12), calls=%async_computation.3 | async-start | bytes 1179648 | tf_op jit(solution)/shard_map/all_to_all | solution.py:34
  78.7 30.0 %all-to-all-start.2 = ((f32[24,4,1280]{2,1,0:T(4,128)}), f32[24,4,1280]{2,1,0:T(4,128)S(1)}, u32[]{:S(2)}, u32[]{:S(2)}) async-start(f32[24,4,1280]{2,1,0:T(4,128)} %reshape.55), calls=%async_computation.2 | async-start | bytes 983040 | tf_op jit(solution)/shard_map/all_to_all | solution.py:34

commit v2 on v1

v2 whole, which is shorter than its diff:
```python
import jax
import jax.numpy as jnp
from jax import lax
from jax.sharding import Mesh
from jax.sharding import PartitionSpec as P

epsilon = 1e-06
AXES = ("x", "yh", "z", "yl", "c")
SIZES = (4, 4, 12, 2, 2)
IMAGE = ("c", "z")
TEXT = ("x", "yh", "yl")
IMAGE_GAIN = 16.0
TEXT_GAIN = 32.0


def unit_rows(embeds):
    values = embeds.astype(jnp.float32)
    inverse = lax.rsqrt(jnp.sum(values * values, axis=1, keepdims=True) + epsilon)
    unit = values * inverse
    return (inverse, unit, unit.astype(jnp.bfloat16))


def backward_unit(inverse, unit, upstream):
    return inverse * (upstream - unit * jnp.sum(unit * upstream, axis=1, keepdims=True))


def share_text(rows):
    count = lax.axis_size(TEXT)
    copies = jnp.broadcast_to(rows[None], (count,) + rows.shape)
    return lax.all_to_all(copies, TEXT, 0, 0, tiled=True).reshape(count * rows.shape[0], -1)


def share_images(rows):
    along_z = lax.all_gather(rows, "z", axis=0, tiled=True)
    return lax.all_gather(along_z, "c", axis=0, tiled=True)


def send_rows(pieces, axes):
    count = lax.axis_size(axes)
    pieces = pieces.reshape(count, pieces.shape[0] // count, pieces.shape[1])
    return lax.all_to_all(pieces, axes, 0, 0, tiled=True)


def sum_rows(arrived, gain):
    return jnp.sum(arrived.astype(jnp.float32), axis=0) * (1.0 / gain)


def on_device(image_embeds, text_embeds, log_scale, bias):
    rows, width = image_embeds.shape
    batch = rows * lax.axis_size(AXES)
    text_inverse, text_unit, text_low = unit_rows(text_embeds)
    image_inverse, image_unit, image_low = unit_rows(image_embeds)
    scale_value = jnp.exp(log_scale[0])
    bias_value = bias[0]
    texts = share_text(text_low)
    images = share_images(image_low)
    row_ids = jnp.arange(images.shape[0], dtype=jnp.int32)[:, None] - rows * lax.axis_index(IMAGE)
    column_ids = jnp.arange(texts.shape[0], dtype=jnp.int32)[None, :] - rows * lax.axis_index(TEXT)
    positive = (row_ids == column_ids) & (row_ids >= 0) & (row_ids < rows)
    raw_logits = lax.dot_general(
        images, texts, (((1,), (1,)), ((), ())), preferred_element_type=jnp.float32
    )
    logits = scale_value * raw_logits + bias_value
    labels = jnp.where(positive, 1.0, -1.0).astype(jnp.float32)
    losses = jnp.sum(jax.nn.softplus(-labels * logits), axis=1, keepdims=True)
    coefs = (-scale_value * labels * jax.nn.sigmoid(-labels * logits)).astype(jnp.bfloat16)
    text_part = lax.dot_general(
        coefs, images, (((0,), (0,)), ((), ())), preferred_element_type=jnp.float32
    )
    text_arrived = send_rows((text_part * TEXT_GAIN).astype(jnp.float16), TEXT)
    image_part = jnp.dot(coefs, texts, preferred_element_type=jnp.float32)
    packed = jnp.concatenate([image_part, jnp.broadcast_to(losses, (losses.shape[0], 128))], axis=1)
    both = lax.all_gather(packed, "c", axis=0).reshape(2, 2, packed.shape[0] // 2, -1)
    chip_part = jnp.sum(lax.dynamic_index_in_dim(both, lax.axis_index("c"), 1, keepdims=False), axis=0)
    chip_loss = chip_part[:, width:]
    rest = chip_loss - (chip_loss * IMAGE_GAIN).astype(jnp.float16).astype(jnp.float32) * (1.0 / IMAGE_GAIN)
    upper = jnp.arange(128, dtype=jnp.int32)[None, :] >= 64
    chip_part = jnp.concatenate([chip_part[:, :width], jnp.where(upper, rest, chip_loss)], axis=1)
    image_pieces = (chip_part * IMAGE_GAIN).astype(jnp.float16)
    image_pieces, text_arrived = lax.optimization_barrier((image_pieces, text_arrived))
    image_sum = sum_rows(send_rows(image_pieces, "z"), IMAGE_GAIN)
    text_sum = sum_rows(text_arrived, TEXT_GAIN)
    row_loss = (image_sum[:, width] + image_sum[:, width + 64]) / batch
    image_grad = backward_unit(image_inverse, image_unit, image_sum[:, :width])
    text_grad = backward_unit(text_inverse, text_unit, text_sum)
    return (row_loss, image_grad, text_grad)


def solution(mesh):
    fine = Mesh(mesh.devices.reshape(SIZES), AXES)
    in_specs = (P(AXES, None), P(AXES, None), P(), P())
    out_specs = (P(AXES), P(AXES, None), P(AXES, None))
    return jax.shard_map(
        on_device, mesh=fine, in_specs=in_specs, out_specs=out_specs, check_vma=False
    )
```

time: 112 us -> 92.7 us (0.83)
  the two profiles are of different devices: /device:TPU:1 before, /device:TPU:8 now
where the time goes in v2:
time: 92.7 us; the launch traced here: 92.2 us
  blocking collectives  34.5 us (37%)
  starting transfers between devices  26.4 us (28%)
  waiting for transfers between devices  21.8 us (24%)
  other arithmetic  3.95 us (4%)
  local copies, waits for them, and re-layouts  2.47 us (3%)
  between operations  2.1 us (2%)
  matrix products  1.02 us (1%)
    all_gather x1, blocking collectives, share_images(): along_z = lax.all_gather(rows, 'z', axis=0, tiled=True)  30 us
    all_to_all x2, waiting for transfers between devices, send_rows(): return lax.all_to_all(pieces, axes, 0, 0, tiled=True)  21.8 us
    all_to_all x2, starting transfers between devices, send_rows(): return lax.all_to_all(pieces, axes, 0, 0, tiled=True)  13.3 us
    all_to_all x1, starting transfers between devices, share_text(): lax.all_to_all(copies, TEXT, 0, 0, tiled=True)  13.1 us
    all_gather x1, blocking collectives, on_device(): lax.all_gather(packed, 'c', axis=0).reshape(2, 2, packed.shape[0] // 2, -1)  2.51 us
    all_gather x1, blocking collectives, share_images(): return lax.all_gather(along_z, 'c', axis=0, tiled=True)  1.97 us
  transfers between devices with their start and end apart: 3, of which 2 were waited for; matrix products, arithmetic and copies ran while one was open for 1% of the time, Pallas kernels for 0%

profile of v2, /device:TPU:8, one launch (start us, length us, event | category | flops | bytes accessed | tf_op | source)
XLA Modules:
  0.0 92.2 jit_solution(5948845123006228114)
XLA Ops:
  0.6 0.0 copy-start
  0.6 0.9 fusion.20
  1.5 0.0 copy-done
  1.5 0.1 fusion.9
  1.6 0.8 broadcast_in_dim.19
  2.4 0.0 copy-start.1
  2.4 13.1 %all-to-all-start = ((bf16[32,4,1152]{2,1,0:T(4,128)(2,1)}), bf16[32,4,1152]{2,1,0:T(4,128)(2,1)S(1)}, u32[]{:S(2)}, u32[]{:S(2)}) async-start(bf16[32,4,1152]{2,1,0:T(4,128)(2,1)} %broadcast_in_dim.19), calls=%async_computation | async-start | bytes 589824 | tf_op jit(solution)/shard_map/all_to_all | solution.py:30
  15.5 0.0 copy-done.1
  15.5 0.1 fusion.16
  15.7 0.1 fusion.21
  15.8 30.0 %all-gather.1 = bf16[12,4,1152]{2,1,0:T(4,128)(2,1)S(1)} all-gather(bf16[1,4,1152]{2,1,0:T(4,128)(2,1)S(1)} %fusion.21), channel_id=1, replica_groups=mesh['x'=4,'yh'=4,'z'=12,'yl'=2,'c'=2] {'z'}, dimensions={0}, use_global_device_ids=true | all-gather | bytes 119808 | tf_op jit(solution)/shard_map/all_gather | solution.py:34
  47.2 2.0 %all_gather.13 = bf16[96,1152]{1,0:T(8,128)(2,1)S(1)} all-gather(bf16[48,1152]{1,0:T(8,128)(2,1)S(1)} %reshape.66), channel_id=1, replica_groups=mesh['x'=4,'yh'=4,'z'=12,'yl'=2,'c'=2] {'c'}, dimensions={0}, use_global_device_ids=true | all-gather | bytes 331776 | tf_op jit(solution)/shard_map/all_gather | solution.py:35
  49.2 0.0 all-to-all-done
  49.2 0.1 reshape.59
  49.3 0.4 fusion.6
  49.6 0.3 fusion.25
  49.9 0.4 fusion
  50.3 0.8 reshape.61
  51.1 9.8 %all-to-all-start.1 = ((f16[32,4,1152]{2,1,0:T(4,128)(2,1)}), f16[32,4,1152]{2,1,0:T(4,128)(2,1)S(1)}, u32[]{:S(2)}, u32[]{:S(2)}) async-start(f16[32,4,1152]{2,1,0:T(4,128)(2,1)} %reshape.61), calls=%async_computation.1 | async-start | bytes 589824 | tf_op jit(solution)/shard_map/all_to_all | solution.py:41
  60.9 0.1 broadcast_in_dim.23
  61.0 2.5 %all-gather = f32[192,1280]{1,0:T(8,128)S(1)} all-gather(f32[96,1280]{1,0:T(8,128)S(1)} %pad_maximum_fusion), channel_id=2, replica_groups=mesh['x'=4,'yh'=4,'z'=12,'yl'=2,'c'=2] {'c'}, dimensions={0}, use_global_device_ids=true | all-gather | bytes 1474560 | tf_op jit(solution)/shard_map/all_gather | solution.py:73
  63.6 10.5 %all-to-all-done.1 = f16[32,4,1152]{2,1,0:T(4,128)(2,1)S(1)} async-done(((f16[32,4,1152]{2,1,0:T(4,128)(2,1)}), f16[32,4,1152]{2,1,0:T(4,128)(2,1)S(1)}, u32[]{:S(2)}, u32[]{:S(2)}) %all-to-all-start.1) | async-done | bytes 294944 | tf_op jit(solution)/shard_map/all_to_all | solution.py:41
  74.1 0.1 convert_reduce_fusion
  74.2 0.2 fusion.17
  74.4 0.7 reshape.62
  75.1 3.5 %all-to-all-start.2 = ((f16[12,4,1280]{2,1,0:T(4,128)(2,1)}), f16[12,4,1280]{2,1,0:T(4,128)(2,1)S(1)}, u32[]{:S(2)}, u32[]{:S(2)}) async-start(f16[12,4,1280]{2,1,0:T(4,128)(2,1)} %reshape.62), calls=%async_computation.2 | async-start | bytes 245760 | tf_op jit(solution)/shard_map/all_to_all | solution.py:41
  78.6 0.7 fusion.19
  79.3 11.2 %all-to-all-done.2 = f16[12,4,1280]{2,1,0:T(4,128)(2,1)S(1)} async-done(((f16[12,4,1280]{2,1,0:T(4,128)(2,1)}), f16[12,4,1280]{2,1,0:T(4,128)(2,1)S(1)}, u32[]{:S(2)}, u32[]{:S(2)}) %all-to-all-start.2) | async-done | bytes 122912 | tf_op jit(solution)/shard_map/all_to_all | solution.py:41
  90.6 0.1 convert_reduce_fusion.1
  90.6 0.2 fusion.13
  90.8 0.7 fusion.23
  91.5 0.7 fusion.15
  (13 shorter events, 0.2 us)
Async XLA Ops:
  0.6 0.9 copy-start
  2.4 13.1 %copy-start.1 = (bf16[4,1152]{1,0:T(4,128)(2,1)S(1)}, bf16[4,1152]{1,0:T(4,128)(2,1)}, u32[]{:S(2)}) copy-start(bf16[4,1152]{1,0:T(4,128)(2,1)} %param.4) | copy-start | bytes 27652
  2.4 46.8 %all-to-all-start = ((bf16[32,4,1152]{2,1,0:T(4,128)(2,1)}), bf16[32,4,1152]{2,1,0:T(4,128)(2,1)S(1)}, u32[]{:S(2)}, u32[]{:S(2)}) async-start(bf16[32,4,1152]{2,1,0:T(4,128)(2,1)} %broadcast_in_dim.19), calls=%async_computation | async-start | bytes 589824 | tf_op jit(solution)/shard_map/all_to_all | solution.py:30
  51.1 23.0 %all-to-all-start.1 = ((f16[32,4,1152]{2,1,0:T(4,128)(2,1)}), f16[32,4,1152]{2,1,0:T(4,128)(2,1)S(1)}, u32[]{:S(2)}, u32[]{:S(2)}) async-start(f16[32,4,1152]{2,1,0:T(4,128)(2,1)} %reshape.61), calls=%async_computation.1 | async-start | bytes 589824 | tf_op jit(solution)/shard_map/all_to_all | solution.py:41
  75.1 15.4 %all-to-all-start.2 = ((f16[12,4,1280]{2,1,0:T(4,128)(2,1)}), f16[12,4,1280]{2,1,0:T(4,128)(2,1)S(1)}, u32[]{:S(2)}, u32[]{:S(2)}) async-start(f16[12,4,1280]{2,1,0:T(4,128)(2,1)} %reshape.62), calls=%async_computation.2 | async-start | bytes 245760 | tf_op jit(solution)/shard_map/all_to_all | solution.py:41

commit v3 on v1

v3 whole, which is shorter than its diff:
```python
import jax
import jax.numpy as jnp
from jax import lax
from jax.sharding import Mesh
from jax.sharding import PartitionSpec as P

epsilon = 1e-06
AXES = ("x", "yh", "z", "yl", "c")
SIZES = (4, 4, 12, 2, 2)
RUN = 3
STRIDE = 2
GAIN = 16.0
LOSS_COLUMNS = 128


def exchange_groups():
    members = {}
    xs, yhs, zs, yls, cs = SIZES
    device = 0
    for x in range(xs):
        for yh in range(yhs):
            for z in range(zs):
                for yl in range(yls):
                    text_key = (0, yh, z // RUN, 0)
                    image_key = (1, x, yl, z % STRIDE)
                    for core, key in enumerate((text_key, image_key)):
                        members.setdefault(key, []).append(device + core)
                    device += cs
    return [members[key] for key in sorted(members)]


def exchange(pieces):
    return lax.all_to_all(pieces, AXES, 0, 0, axis_index_groups=exchange_groups(), tiled=True)


def on_device(image_embeds, text_embeds, log_scale, bias):
    rows, width = image_embeds.shape
    batch = rows * lax.axis_size(AXES)
    x, yh, z, yl, c = [lax.axis_index(name) for name in AXES]
    is_text = c == 0
    chip_rows = 2 * rows
    chip_embeds = lax.all_gather(jnp.concatenate([text_embeds, image_embeds], axis=0), "c", axis=0)
    embeds = jnp.where(is_text, chip_embeds[:, :rows], chip_embeds[:, rows:]).reshape(chip_rows, width)
    values = embeds.astype(jnp.float32)
    inverse = lax.rsqrt(jnp.sum(values * values, axis=1, keepdims=True) + epsilon)
    unit = values * inverse
    low = unit.astype(jnp.bfloat16)
    scale_value = jnp.exp(log_scale[0])
    bias_value = bias[0]
    count = len(exchange_groups()[0])
    own = exchange(jnp.broadcast_to(low[None], (count, chip_rows, width))).reshape(-1, width)
    both = lax.all_gather(own, "c", axis=0)
    other = jnp.where(is_text, both[1], both[0])
    text_place = (x * RUN + z % RUN) * 2 + yl
    image_place = yh * (SIZES[2] // STRIDE) + z // STRIDE
    own_place = jnp.where(is_text, text_place, image_place)
    other_place = jnp.where(is_text, image_place, text_place)
    own_step = jnp.where(is_text, 2 * STRIDE, 1)
    other_step = jnp.where(is_text, 1, 2 * STRIDE)
    own_ids = jnp.arange(own.shape[0], dtype=jnp.int32)[:, None] - chip_rows * own_place
    other_ids = jnp.arange(own.shape[0], dtype=jnp.int32)[None, :] - chip_rows * other_place
    own_twin = own_ids - chip_rows * own_step
    other_twin = other_ids - chip_rows * other_step
    positive = ((own_ids == other_ids) & (own_ids >= 0) & (own_ids < chip_rows)) | (
        (z % RUN == 0) & (own_twin == other_twin) & (own_twin >= 0) & (own_twin < chip_rows)
    )
    counted = jnp.where(z % RUN == RUN - 1, 0.0, 1.0)
    raw_logits = lax.dot_general(
        own, other, (((1,), (1,)), ((), ())), preferred_element_type=jnp.float32
    )
    logits = scale_value * raw_logits + bias_value
    labels = jnp.where(positive, 1.0, -1.0).astype(jnp.float32)
    losses = counted * jnp.sum(jax.nn.softplus(-labels * logits), axis=1, keepdims=True)
    coefs = (-scale_value * counted * labels * jax.nn.sigmoid(-labels * logits)).astype(jnp.bfloat16)
    part = jnp.dot(coefs, other, preferred_element_type=jnp.float32) * GAIN
    losses = losses * GAIN
    rest = losses - losses.astype(jnp.float16).astype(jnp.float32)
    upper = jnp.arange(LOSS_COLUMNS, dtype=jnp.int32)[None, :] >= LOSS_COLUMNS // 2
    packed = jnp.concatenate([part, jnp.where(upper, rest, losses)], axis=1).astype(jnp.float16)
    arrived = exchange(packed.reshape(count, chip_rows, -1))
    total = jnp.sum(arrived.astype(jnp.float32), axis=0) * (1.0 / GAIN)
    upstream = total[:, :width]
    row_loss = (total[:, width:] + jnp.roll(total[:, width:], LOSS_COLUMNS // 2, axis=1)) / batch
    grad = inverse * (upstream - unit * jnp.sum(unit * upstream, axis=1, keepdims=True))
    chip_grads = lax.all_gather(jnp.concatenate([grad, row_loss], axis=1), "c", axis=0)
    text_out = lax.dynamic_slice_in_dim(chip_grads[0], c * rows, rows, 0)
    image_out = lax.dynamic_slice_in_dim(chip_grads[1], c * rows, rows, 0)
    return (image_out[:, width], image_out[:, :width], text_out[:, :width])


def solution(mesh):
    fine = Mesh(mesh.devices.reshape(SIZES), AXES)
    in_specs = (P(AXES, None), P(AXES, None), P(), P())
    out_specs = (P(AXES), P(AXES, None), P(AXES, None))
    return jax.shard_map(
        on_device, mesh=fine, in_specs=in_specs, out_specs=out_specs, check_vma=False
    )
```

time: 112 us -> 75 us (0.67)
  starting transfers between devices: 42.7 us -> 15.8 us
  waiting for transfers between devices: 56.6 us -> 33.6 us
  blocking collectives: 0 us -> 16.3 us
  other arithmetic: 3.94 us -> 2.41 us
    all_to_all x4 -> x2, starting transfers between devices: 42.7 us -> 15.8 us  [exchange(): lax.all_to_all(pieces, AXES, 0, 0, axis_index_groups=exchange_groups(), t...]
    all_to_all x4 -> x2, waiting for transfers between devices: 56.6 us -> 33.6 us  [exchange(): lax.all_to_all(pieces, AXES, 0, 0, axis_index_groups=exchange_groups(), t...]
    all_gather x0 -> x3, blocking collectives: none -> 16.3 us  [the longest x1 12 us: on_device(): lax.all_gather(jnp.concatenate([text_embeds, image_embeds], axis=0), 'c',...]
    slice x0 -> x5, local copies, waits for them, and re-layouts: none -> 2 us  [the longest x3 1.92 us: on_device(): return (image_out[:, width], image_out[:, :width], text_out[:, :width])]
    concatenate x1 -> x3, other arithmetic: 0.04 us -> 1.63 us  [the longest x1 0.9 us: on_device(): jnp.concatenate([part, jnp.where(upper, rest, losses)], axis=1)]
    mul x2 -> x3, other arithmetic: 1.37 us -> 0.09 us  [the longest x1 0.08 us: on_device(): inverse * (upstream - unit * jnp.sum(unit * upstream, axis=1, keepdims=Tr...]
    reduce_sum x6 -> x3, other arithmetic: 1.58 us -> 0.37 us  [the longest x1 0.19 us: on_device(): jnp.sum(unit * upstream, axis=1, keepdims=True)]
    dot_general x1 -> x0, local copies, waits for them, and re-layouts: 1.19 us -> none  [on_device(): lax.dot_general(coefs, images, (((0,), (0,)), ((), ())), preferred_elemen...]
  transfers between devices with their start and end apart: 4 -> 2, of which waited for: 4 -> 2; matrix products, arithmetic and copies ran while one was open for 2% -> 0% of each run, Pallas kernels for 0% -> 0%
where the time goes in v3:
time: 75 us; the launch traced here: 74.3 us
  waiting for transfers between devices  33.6 us (45%)
  blocking collectives  16.3 us (22%)
  starting transfers between devices  15.8 us (21%)
  local copies, waits for them, and re-layouts  2.98 us (4%)
  other arithmetic  2.41 us (3%)
  between operations  2.14 us (3%)
  matrix products  0.98 us (1%)
    all_to_all x2, waiting for transfers between devices, exchange(): lax.all_to_all(pieces, AXES, 0, 0, axis_index_groups=exchange_groups(), t...  33.6 us
    all_to_all x2, starting transfers between devices, exchange(): lax.all_to_all(pieces, AXES, 0, 0, axis_index_groups=exchange_groups(), t...  15.8 us
    all_gather x1, blocking collectives, on_device(): lax.all_gather(jnp.concatenate([text_embeds, image_embeds], axis=0), 'c',...  12 us
    all_gather x1, blocking collectives, on_device(): both = lax.all_gather(own, 'c', axis=0)  2.43 us
    slice x3, local copies, waits for them, and re-layouts, on_device(): return (image_out[:, width], image_out[:, :width], text_out[:, :width])  1.92 us
    all_gather x1, blocking collectives, on_device(): lax.all_gather(jnp.concatenate([grad, row_loss], axis=1), 'c', axis=0)  1.85 us
  transfers between devices with their start and end apart: 2, of which 2 were waited for; matrix products, arithmetic and copies ran while one was open for 0% of the time, Pallas kernels for 0%

profile of v3, /device:TPU:1, one launch (start us, length us, event | category | flops | bytes accessed | tf_op | source)
XLA Modules:
  0.0 74.3 jit_solution(4968439636858099416)
XLA Ops:
  0.6 0.7 pad_maximum_fusion.2
  1.4 12.0 %all-gather = bf16[16,1152]{1,0:T(8,128)(2,1)S(1)} all-gather(bf16[8,1152]{1,0:T(8,128)(2,1)S(1)} %pad_maximum_fusion.2), channel_id=2, replica_groups=mesh['x'=4,'yh'=4,'z'=12,'yl'=2,'c'=2] {'c'}, dimensions={0}, use_global_device_ids=true | all-gather | bytes 55296 | tf_op jit(solution)/shard_map/all_gather | solution.py:42
  13.4 0.1 multiply_reduce_fusion.1
  13.5 0.1 rsqrt.12
  13.6 0.1 multiply_convert_fusion
  13.7 0.8 %broadcast_in_dim.46 = bf16[24,8,1152]{2,1,0:T(8,128)(2,1)} broadcast(bf16[8,1152]{1,0:T(8,128)(2,1)S(1)} %multiply_convert_fusion), dimensions={1,2} | broadcast | bytes 460800 | tf_op jit(solution)/shard_map/broadcast_in_dim | solution.py:51
  14.5 10.7 %all-to-all-start = ((bf16[24,8,1152]{2,1,0:T(8,128)(2,1)}), bf16[24,8,1152]{2,1,0:T(8,128)(2,1)S(1)}, u32[]{:S(2)}, u32[]{:S(2)}) async-start(bf16[24,8,1152]{2,1,0:T(8,128)(2,1)} %broadcast_in_dim.46), calls=%async_computation | async-start | bytes 884736 | tf_op jit(solution)/shard_map/all_to_all | solution.py:33
  26.7 16.1 %all-to-all-done = bf16[24,8,1152]{2,1,0:T(8,128)(2,1)S(1)} async-done(((bf16[24,8,1152]{2,1,0:T(8,128)(2,1)}), bf16[24,8,1152]{2,1,0:T(8,128)(2,1)S(1)}, u32[]{:S(2)}, u32[]{:S(2)}) %all-to-all-start) | async-done | bytes 442400 | tf_op jit(solution)/shard_map/all_to_all | solution.py:33
  42.7 2.4 %all_gather.17 = bf16[2,192,1152]{2,1,0:T(8,128)(2,1)S(1)} all-gather(bf16[1,192,1152]{2,1,0:T(8,128)(2,1)S(1)} %bitcast.18), channel_id=1, replica_groups=mesh['x'=4,'yh'=4,'z'=12,'yl'=2,'c'=2] {'c'}, dimensions={0}, use_global_device_ids=true | all-gather | bytes 1327104 | tf_op jit(solution)/shard_map/all_gather | solution.py:52
  45.2 0.5 fusion.8
  45.7 0.1 mul.151
  45.8 0.5 fusion.1
  46.3 0.1 select_convert_fusion
  46.4 0.9 %pad_maximum_fusion = f16[24,8,1280]{2,1,0:T(8,128)(2,1)} fusion(f16[24,8,128]{2,1,0:T(8,128)(2,1)S(1)} %select_convert_fusion, f16[24,8,1152]{2,1,0:T(8,128)(2,1)S(1)} %fusion.1), kind=kLoop, calls=%fused_computation.8 | loop fusion | flops 245760 | bytes 983040 | tf_op jit(solution)/shard_map/concatenate | solution.py:79
  47.3 5.1 %all-to-all-start.1 = ((f16[24,8,1280]{2,1,0:T(8,128)(2,1)}), f16[24,8,1280]{2,1,0:T(8,128)(2,1)S(1)}, u32[]{:S(2)}, u32[]{:S(2)}) async-start(f16[24,8,1280]{2,1,0:T(8,128)(2,1)} %pad_maximum_fusion), calls=%async_computation.1 | async-start | bytes 983040 | tf_op jit(solution)/shard_map/all_to_all | solution.py:33
  52.4 17.6 %all-to-all-done.1 = f16[24,8,1280]{2,1,0:T(8,128)(2,1)S(1)} async-done(((f16[24,8,1280]{2,1,0:T(8,128)(2,1)}), f16[24,8,1280]{2,1,0:T(8,128)(2,1)S(1)}, u32[]{:S(2)}, u32[]{:S(2)}) %all-to-all-start.1) | async-done | bytes 491552 | tf_op jit(solution)/shard_map/all_to_all | solution.py:33
  69.9 0.1 convert_reduce_fusion
  70.0 0.2 multiply_reduce_fusion
  70.2 0.1 fusion.24
  70.3 0.1 subtract_multiply_fusion
  70.4 0.1 fusion.16
  70.5 1.9 %all-gather.1 = f32[16,1280]{1,0:T(8,128)S(1)} all-gather(f32[8,1280]{1,0:T(8,128)S(1)} %pad_maximum_fusion.1), channel_id=3, replica_groups=mesh['x'=4,'yh'=4,'z'=12,'yl'=2,'c'=2] {'c'}, dimensions={0}, use_global_device_ids=true | all-gather | bytes 122880 | tf_op jit(solution)/shard_map/all_gather | solution.py:85
  72.3 0.6 constant_dynamic-slice_fusion
  72.9 0.6 constant_dynamic-slice_fusion.1
  73.6 0.7 dynamic-slice_reduce_fusion
  (12 shorter events, 0.1 us)
Async XLA Ops:
  14.5 28.3 %all-to-all-start = ((bf16[24,8,1152]{2,1,0:T(8,128)(2,1)}), bf16[24,8,1152]{2,1,0:T(8,128)(2,1)S(1)}, u32[]{:S(2)}, u32[]{:S(2)}) async-start(bf16[24,8,1152]{2,1,0:T(8,128)(2,1)} %broadcast_in_dim.46), calls=%async_computation | async-start | bytes 884736 | tf_op jit(solution)/shard_map/all_to_all | solution.py:33
  47.3 22.7 %all-to-all-start.1 = ((f16[24,8,1280]{2,1,0:T(8,128)(2,1)}), f16[24,8,1280]{2,1,0:T(8,128)(2,1)S(1)}, u32[]{:S(2)}, u32[]{:S(2)}) async-start(f16[24,8,1280]{2,1,0:T(8,128)(2,1)} %pad_maximum_fusion), calls=%async_computation.1 | async-start | bytes 983040 | tf_op jit(solution)/shard_map/all_to_all | solution.py:33

commit v4 on v3

v4 whole, which is shorter than its diff:
```python
import jax
import jax.numpy as jnp
from jax import lax
from jax.sharding import Mesh
from jax.experimental import pallas as pl
from jax.experimental.pallas import tpu as pltpu
from jax.sharding import PartitionSpec as P

epsilon = 1e-06
AXES = ("x", "yh", "z", "yl", "c")
SIZES = (4, 4, 12, 2, 2)
SLAB = 3
GAIN = 16.0
LOSS_COLUMNS = 128


def device_place(device):
    coordinates = []
    for size in reversed(SIZES):
        coordinates.append(device % size)
        device = device // size
    return coordinates[::-1]


def places(x, y, z):
    plane = z % SLAB
    text_place = 2 * z + x % 2
    outer_place = 8 * (x // 2) + y
    middle_place = 16 + 4 * (x // 2) + y // 2
    return (plane, text_place, outer_place, middle_place)


def exchange_groups():
    members = {}
    xs, yhs, zs, yls, cs = SIZES
    device = 0
    for x in range(xs):
        for yh in range(yhs):
            for z in range(zs):
                for yl in range(yls):
                    y = yh * yls + yl
                    plane, text_place, outer_place, middle_place = places(x, y, z)
                    last = (x // 2 + y) % 2 if plane == 1 else plane // 2
                    image_place = middle_place if plane == 1 else outer_place
                    text_key = (0, x // 2, y, 0)
                    image_key = (1, z // SLAB, last, x % 2)
                    for core, key, place in ((0, text_key, text_place), (1, image_key, image_place)):
                        members.setdefault(key, []).append((place, device + core))
                    device += cs
    return [[device for _, device in sorted(members[key])] for key in sorted(members)]


def exchange(pieces):
    return lax.all_to_all(pieces, AXES, 0, 0, axis_index_groups=exchange_groups(), tiled=True)


def on_device(image_embeds, text_embeds, log_scale, bias):
    rows, width = image_embeds.shape
    batch = rows * lax.axis_size(AXES)
    device = lax.axis_index(AXES)
    is_text = device % SIZES[-1] == 0
    chip_rows = 2 * rows
    chip_embeds = lax.all_gather(jnp.concatenate([text_embeds, image_embeds], axis=0), "c", axis=0)
    embeds = jnp.where(is_text, chip_embeds[:, :rows], chip_embeds[:, rows:]).reshape(chip_rows, width)
    values = embeds.astype(jnp.float32)
    inverse = lax.rsqrt(jnp.sum(values * values, axis=1, keepdims=True) + epsilon)
    unit = values * inverse
    low = unit.astype(jnp.bfloat16)
    count = len(exchange_groups()[0])
    pieces = jnp.broadcast_to(low[None], (count, chip_rows, width))
    half_columns = jnp.int32(LOSS_COLUMNS // 2)
    tied = lax.optimization_barrier((pieces, device, log_scale, bias, half_columns))
    own, device, log_scale, bias, half_columns = lax.optimization_barrier(
        (exchange(tied[0]),) + tied[1:]
    )
    scale_value = jnp.exp(log_scale[0])
    bias_value = bias[0]
    x, yh, z, yl, c = device_place(device)
    own_is_text = c == 0
    own = own.reshape(-1, width)
    both = lax.all_gather(own, "c", axis=0)
    other = jnp.where(own_is_text, both[1], both[0])
    y = yh * SIZES[3] + yl
    plane, text_place, image_place, twin_image_place = places(x, y, z)
    twin_text_place = text_place + jnp.where(plane == 0, 2, -2)
    has_twin = plane // 2 == (x // 2 + y) % 2

    def row_ids(place, axis):
        return lax.broadcasted_iota(jnp.int32, (own.shape[0], own.shape[0]), axis) - chip_rows * place

    def same_rows(text, image):
        own_ids = row_ids(jnp.where(own_is_text, text, image), 0)
        other_ids = row_ids(jnp.where(own_is_text, image, text), 1)
        return (own_ids == other_ids) & (own_ids >= 0) & (own_ids < chip_rows)

    positive = same_rows(text_place, image_place) | (
        has_twin & same_rows(twin_text_place, twin_image_place)
    )
    counted = jnp.where(plane == 1, 0.0, 1.0)
    raw_logits = lax.dot_general(
        own, other, (((1,), (1,)), ((), ())), preferred_element_type=jnp.float32
    )
    logits = scale_value * raw_logits + bias_value
    labels = jnp.where(positive, 1.0, -1.0).astype(jnp.float32)
    losses = counted * jnp.sum(jax.nn.softplus(-labels * logits), axis=1, keepdims=True)
    coefs = (-scale_value * counted * labels * jax.nn.sigmoid(-labels * logits)).astype(jnp.bfloat16)
    part = jnp.dot(coefs, other, preferred_element_type=jnp.float32) * GAIN
    losses = losses * GAIN
    rest = losses - losses.astype(jnp.float16).astype(jnp.float32)
    upper = jnp.arange(LOSS_COLUMNS, dtype=jnp.int32)[None, :] >= half_columns
    packed = jnp.concatenate([part, jnp.where(upper, rest, losses)], axis=1).astype(jnp.float16)
    arrived = exchange(packed.reshape(count, chip_rows, -1))
    total = jnp.sum(arrived.astype(jnp.float32), axis=0) * (1.0 / GAIN)
    upstream = total[:, :width]
    row_loss = (total[:, width:] + jnp.roll(total[:, width:], LOSS_COLUMNS // 2, axis=1)) / batch
    grad = inverse * (upstream - unit * jnp.sum(unit * upstream, axis=1, keepdims=True))
    chip_grads = lax.all_gather(jnp.concatenate([grad, row_loss], axis=1), "c", axis=0)
    row_loss, image_grad, text_grad = deal_rows(chip_grads, rows, width)
    return (row_loss.reshape(rows), image_grad, text_grad)


def deal_kernel(chip_ref, loss_ref, image_ref, text_ref):
    rows, width = image_ref.shape
    core = lax.axis_index("c")
    for kind, out_ref in ((0, text_ref), (1, image_ref)):
        out_ref[...] = jnp.where(
            core == 0, chip_ref[kind, :rows, :width], chip_ref[kind, rows:, :width]
        )
    losses = chip_ref[1, :, width:]
    row = lax.broadcasted_iota(jnp.int32, losses.shape, 0)
    column = lax.broadcasted_iota(jnp.int32, losses.shape, 1)
    turned = jnp.sum(jnp.where(row == column + rows * core, losses, 0.0), axis=0, keepdims=True)
    loss_ref[...] = turned[:, :rows]


def deal_rows(chip_grads, rows, width):
    return pl.pallas_call(
        deal_kernel,
        in_specs=[pl.BlockSpec(memory_space=pltpu.VMEM)],
        out_specs=[pl.BlockSpec(memory_space=pltpu.VMEM)] * 3,
        out_shape=[
            jax.ShapeDtypeStruct((1, rows), jnp.float32),
            jax.ShapeDtypeStruct((rows, width), jnp.float32),
            jax.ShapeDtypeStruct((rows, width), jnp.float32),
        ],
        compiler_params=pltpu.CompilerParams(vmem_limit_bytes=2 << 20),
        name="deal_rows",
    )(chip_grads)


def solution(mesh):
    fine = Mesh(mesh.devices.reshape(SIZES), AXES)
    in_specs = (P(AXES, None), P(AXES, None), P(), P())
    out_specs = (P(AXES), P(AXES, None), P(AXES, None))
    return jax.shard_map(
        on_device, mesh=fine, in_specs=in_specs, out_specs=out_specs, check_vma=False
    )
```

time: 75 us -> 72.8 us (0.971)
  blocking collectives: 16.3 us -> 52.9 us
  waiting for transfers between devices: 33.6 us -> 9.25 us
  starting transfers between devices: 15.8 us -> 3.86 us
  other arithmetic: 2.41 us -> 0.91 us
  local copies, waits for them, and re-layouts: 2.98 us -> 1.74 us
    all_to_all x0 -> x1, blocking collectives: none -> 25.7 us  [exchange(): lax.all_to_all(pieces, AXES, 0, 0, axis_index_groups=exchange_groups(), t...]
    all_to_all x2 -> x1, waiting for transfers between devices: 33.6 us -> 9.25 us  [exchange(): lax.all_to_all(pieces, AXES, 0, 0, axis_index_groups=exchange_groups(), t...]
    all_to_all x2 -> x1, starting transfers between devices: 15.8 us -> 3.86 us  [exchange(): lax.all_to_all(pieces, AXES, 0, 0, axis_index_groups=exchange_groups(), t...]
    all_gather x1, blocking collectives: 2.43 us -> 11.3 us  [on_device(): both = lax.all_gather(own, 'c', axis=0)]
    all_gather x1, blocking collectives: 1.85 us -> 3.9 us  [on_device(): lax.all_gather(jnp.concatenate([grad, row_loss], axis=1), 'c', axis=0)]
    slice x4 -> x0, local copies, waits for them, and re-layouts: 1.93 us -> none  [the longest x3 1.92 us: on_device(): return (image_out[:, width], image_out[:, :width], text_out[:, :width])]
    concatenate x1, other arithmetic: 0.9 us -> 0.12 us  [on_device(): jnp.concatenate([part, jnp.where(upper, rest, losses)], axis=1)]
  transfers between devices with their start and end apart: 2 -> 1, of which waited for: 2 -> 1; matrix products, arithmetic and copies ran while one was open for 0% -> 0% of each run, Pallas kernels for 0% -> 0%
where the time goes in v4:
time: 72.8 us; the launch traced here: 72.4 us
  blocking collectives  52.9 us (73%)
  waiting for transfers between devices  9.25 us (13%)
  starting transfers between devices  3.86 us (5%)
  between operations  2.14 us (3%)
  local copies, waits for them, and re-layouts  1.74 us (2%)
  matrix products  0.98 us (1%)
  other arithmetic  0.91 us (1%)
    all_to_all x1, blocking collectives, exchange(): lax.all_to_all(pieces, AXES, 0, 0, axis_index_groups=exchange_groups(), t...  25.7 us
    all_gather x1, blocking collectives, on_device(): lax.all_gather(jnp.concatenate([text_embeds, image_embeds], axis=0), 'c',...  12 us
    all_gather x1, blocking collectives, on_device(): both = lax.all_gather(own, 'c', axis=0)  11.3 us
    all_to_all x1, waiting for transfers between devices, exchange(): lax.all_to_all(pieces, AXES, 0, 0, axis_index_groups=exchange_groups(), t...  9.25 us
    all_gather x1, blocking collectives, on_device(): lax.all_gather(jnp.concatenate([grad, row_loss], axis=1), 'c', axis=0)  3.9 us
    all_to_all x1, starting transfers between devices, exchange(): lax.all_to_all(pieces, AXES, 0, 0, axis_index_groups=exchange_groups(), t...  3.86 us
  transfers between devices with their start and end apart: 1, of which 1 were waited for; matrix products, arithmetic and copies ran while one was open for 0% of the time, Pallas kernels for 0%

profile of v4, /device:TPU:1, one launch (start us, length us, event | category | flops | bytes accessed | tf_op | source)
XLA Modules:
  0.0 72.4 jit_solution(12313190017497202164)
XLA Ops:
  0.7 0.0 copy-start.1
  0.7 0.0 copy-start
  0.7 0.7 copy-done.1
  1.4 0.0 copy-done
  1.4 12.0 %all-gather = bf16[16,1152]{1,0:T(8,128)(2,1)S(1)} all-gather(bf16[8,1152]{1,0:T(8,128)(2,1)S(1)} %pad_maximum_fusion.2), channel_id=2, replica_groups=mesh['x'=4,'yh'=4,'z'=12,'yl'=2,'c'=2] {'c'}, dimensions={0}, use_global_device_ids=true | all-gather | bytes 55296 | tf_op jit(solution)/shard_map/all_gather | solution.py:63
  13.4 0.1 multiply_reduce_fusion.1
  13.5 0.1 rsqrt.12
  13.6 0.1 multiply_convert_fusion
  13.7 0.8 %broadcast_in_dim.42 = bf16[24,8,1152]{2,1,0:T(8,128)(2,1)} broadcast(bf16[8,1152]{1,0:T(8,128)(2,1)S(1)} %multiply_convert_fusion), dimensions={1,2} | broadcast | bytes 460800 | tf_op jit(solution)/shard_map/broadcast_in_dim | solution.py:70
  14.5 3.9 %all-to-all-start = ((bf16[24,8,1152]{2,1,0:T(8,128)(2,1)}), bf16[24,8,1152]{2,1,0:T(8,128)(2,1)S(1)}, u32[]{:S(2)}, u32[]{:S(2)}) async-start(bf16[24,8,1152]{2,1,0:T(8,128)(2,1)} %broadcast_in_dim.42), calls=%async_computation | async-start | bytes 884736 | tf_op jit(solution)/shard_map/all_to_all | solution.py:54
  19.7 9.3 %all-to-all-done = bf16[24,8,1152]{2,1,0:T(8,128)(2,1)S(1)} async-done(((bf16[24,8,1152]{2,1,0:T(8,128)(2,1)}), bf16[24,8,1152]{2,1,0:T(8,128)(2,1)S(1)}, u32[]{:S(2)}, u32[]{:S(2)}) %all-to-all-start) | async-done | bytes 442400 | tf_op jit(solution)/shard_map/all_to_all | solution.py:54
  29.0 11.3 %all_gather.17 = bf16[2,192,1152]{2,1,0:T(8,128)(2,1)S(1)} all-gather(bf16[1,192,1152]{2,1,0:T(8,128)(2,1)S(1)} %bitcast.21), channel_id=1, replica_groups=mesh['x'=4,'yh'=4,'z'=12,'yl'=2,'c'=2] {'c'}, dimensions={0}, use_global_device_ids=true | all-gather | bytes 1327104 | tf_op jit(solution)/shard_map/all_gather | solution.py:81
  40.3 0.5 fusion.8
  40.8 0.1 mul.167
  41.0 0.5 fusion.1
  41.4 0.1 select_convert_fusion
  41.6 0.1 pad_maximum_fusion
  41.7 25.7 %all_to_all.10 = f16[24,8,1280]{2,1,0:T(8,128)(2,1)S(1)} all-to-all(f16[24,8,1280]{2,1,0:T(8,128)(2,1)S(1)} %pad_maximum_fusion), channel_id=1, replica_groups={{0,192,4,196,8,200,12,204,16,208,20,212,24,216,28,220,32,224,36,228,40,..., dimensions={0} | all-to-all | bytes 983040 | tf_op jit(solution)/shard_map/all_to_all | solution.py:54
  67.4 0.1 convert_reduce_fusion
  67.5 0.2 multiply_reduce_fusion
  67.7 0.1 fusion.24
  67.7 0.1 subtract_multiply_fusion
  67.8 0.1 fusion.16
  67.9 3.9 %all-gather.1 = f32[16,1280]{1,0:T(8,128)S(1)} all-gather(f32[8,1280]{1,0:T(8,128)S(1)} %pad_maximum_fusion.1), channel_id=3, replica_groups=mesh['x'=4,'yh'=4,'z'=12,'yl'=2,'c'=2] {'c'}, dimensions={0}, use_global_device_ids=true | all-gather | bytes 122880 | tf_op jit(solution)/shard_map/all_gather | solution.py:117
  71.8 0.6 deal_rows.1
  (12 shorter events, 0.1 us)
Async XLA Ops:
  0.7 0.7 copy-start.1
  0.7 0.7 copy-start
  14.5 14.5 %all-to-all-start = ((bf16[24,8,1152]{2,1,0:T(8,128)(2,1)}), bf16[24,8,1152]{2,1,0:T(8,128)(2,1)S(1)}, u32[]{:S(2)}, u32[]{:S(2)}) async-start(bf16[24,8,1152]{2,1,0:T(8,128)(2,1)} %broadcast_in_dim.42), calls=%async_computation | async-start | bytes 884736 | tf_op jit(solution)/shard_map/all_to_all | solution.py:54

commit v5 on v4

--- a/solution.py
+++ b/solution.py
@@ -9,7 +9,7 @@
 epsilon = 1e-06
 AXES = ("x", "yh", "z", "yl", "c")
 SIZES = (4, 4, 12, 2, 2)
-SLAB = 3
+RUN = 3
 GAIN = 16.0
 LOSS_COLUMNS = 128
 
@@ -23,11 +23,12 @@
 
 
 def places(x, y, z):
-    plane = z % SLAB
-    text_place = 2 * z + x % 2
-    outer_place = 8 * (x // 2) + y
-    middle_place = 16 + 4 * (x // 2) + y // 2
-    return (plane, text_place, outer_place, middle_place)
+    run, step = z // RUN, z % RUN
+    last, late = step // 2, run // 2
+    half = (last + late) % 2
+    text_place = RUN * y + step
+    rank = last * (run + 2 * late) + (1 - last) * (2 * run - 2 * late + step)
+    return (step, half, text_place, 6 * x + rank)
 
 
 def exchange_groups():
@@ -39,11 +40,9 @@
             for z in range(zs):
                 for yl in range(yls):
                     y = yh * yls + yl
-                    plane, text_place, outer_place, middle_place = places(x, y, z)
-                    last = (x // 2 + y) % 2 if plane == 1 else plane // 2
-                    image_place = middle_place if plane == 1 else outer_place
-                    text_key = (0, x // 2, y, 0)
-                    image_key = (1, z // SLAB, last, x % 2)
+                    _, half, text_place, image_place = places(x, y, z)
+                    text_key = (0, x, z // RUN)
+                    image_key = (1, y, half)
                     for core, key, place in ((0, text_key, text_place), (1, image_key, image_place)):
                         members.setdefault(key, []).append((place, device + core))
                     device += cs
@@ -80,10 +79,8 @@
     own = own.reshape(-1, width)
     both = lax.all_gather(own, "c", axis=0)
     other = jnp.where(own_is_text, both[1], both[0])
-    y = yh * SIZES[3] + yl
-    plane, text_place, image_place, twin_image_place = places(x, y, z)
-    twin_text_place = text_place + jnp.where(plane == 0, 2, -2)
-    has_twin = plane // 2 == (x // 2 + y) % 2
+    step, _, text_place, image_place = places(x, yh * SIZES[3] + yl, z)
+    has_twin = step == 0
 
     def row_ids(place, axis):
         return lax.broadcasted_iota(jnp.int32, (own.shape[0], own.shape[0]), axis) - chip_rows * place
@@ -94,9 +91,9 @@
         return (own_ids == other_ids) & (own_ids >= 0) & (own_ids < chip_rows)
 
     positive = same_rows(text_place, image_place) | (
-        has_twin & same_rows(twin_text_place, twin_image_place)
+        has_twin & same_rows(text_place + 1, image_place + 1)
     )
-    counted = jnp.where(plane == 1, 0.0, 1.0)
+    counted = jnp.where(step == 1, 0.0, 1.0)
     raw_logits = lax.dot_general(
         own, other, (((1,), (1,)), ((), ())), preferred_element_type=jnp.float32
     )

time: 72.8 us -> 71.5 us (0.982)
  blocking collectives: 52.9 us -> 42.7 us
  waiting for transfers between devices: 9.25 us -> 14.7 us
  starting transfers between devices: 3.86 us -> 7.37 us
    all_gather x1, blocking collectives: 11.3 us -> 2.44 us  [on_device(): both = lax.all_gather(own, 'c', axis=0)]
    all_to_all x1, waiting for transfers between devices: 9.25 us -> 14.7 us  [exchange(): lax.all_to_all(pieces, AXES, 0, 0, axis_index_groups=exchange_groups(), t...]
    all_to_all x1, starting transfers between devices: 3.86 us -> 7.37 us  [exchange(): lax.all_to_all(pieces, AXES, 0, 0, axis_index_groups=exchange_groups(), t...]
    all_gather x1, blocking collectives: 3.9 us -> 1.85 us  [on_device(): lax.all_gather(jnp.concatenate([grad, row_loss], axis=1), 'c', axis=0)]
where the time goes in v5:
time: 71.5 us; the launch traced here: 71.1 us
  blocking collectives  42.7 us (60%)
  waiting for transfers between devices  14.7 us (21%)
  starting transfers between devices  7.37 us (10%)
  between operations  2.11 us (3%)
  local copies, waits for them, and re-layouts  1.74 us (2%)
  matrix products  0.98 us (1%)
  other arithmetic  0.91 us (1%)
    all_to_all x1, blocking collectives, exchange(): lax.all_to_all(pieces, AXES, 0, 0, axis_index_groups=exchange_groups(), t...  26.4 us
    all_to_all x1, waiting for transfers between devices, exchange(): lax.all_to_all(pieces, AXES, 0, 0, axis_index_groups=exchange_groups(), t...  14.7 us
    all_gather x1, blocking collectives, on_device(): lax.all_gather(jnp.concatenate([text_embeds, image_embeds], axis=0), 'c',...  12 us
    all_to_all x1, starting transfers between devices, exchange(): lax.all_to_all(pieces, AXES, 0, 0, axis_index_groups=exchange_groups(), t...  7.37 us
    all_gather x1, blocking collectives, on_device(): both = lax.all_gather(own, 'c', axis=0)  2.44 us
    all_gather x1, blocking collectives, on_device(): lax.all_gather(jnp.concatenate([grad, row_loss], axis=1), 'c', axis=0)  1.85 us
  transfers between devices with their start and end apart: 1, of which 1 were waited for; matrix products, arithmetic and copies ran while one was open for 0% of the time, Pallas kernels for 0%

profile of v5, /device:TPU:1, one launch (start us, length us, event | category | flops | bytes accessed | tf_op | source)
XLA Modules:
  0.0 71.1 jit_solution(12277669088194940087)
XLA Ops:
  0.7 0.0 copy-start.1
  0.7 0.0 copy-start
  0.7 0.7 copy-done.1
  1.4 0.0 copy-done
  1.4 12.0 %all-gather = bf16[16,1152]{1,0:T(8,128)(2,1)S(1)} all-gather(bf16[8,1152]{1,0:T(8,128)(2,1)S(1)} %pad_maximum_fusion.2), channel_id=2, replica_groups=mesh['x'=4,'yh'=4,'z'=12,'yl'=2,'c'=2] {'c'}, dimensions={0}, use_global_device_ids=true | all-gather | bytes 55296 | tf_op jit(solution)/shard_map/all_gather | solution.py:62
  13.4 0.1 multiply_reduce_fusion.1
  13.5 0.1 rsqrt.12
  13.6 0.1 multiply_convert_fusion
  13.7 0.8 %broadcast_in_dim.42 = bf16[24,8,1152]{2,1,0:T(8,128)(2,1)} broadcast(bf16[8,1152]{1,0:T(8,128)(2,1)S(1)} %multiply_convert_fusion), dimensions={1,2} | broadcast | bytes 460800 | tf_op jit(solution)/shard_map/broadcast_in_dim | solution.py:69
  14.5 7.4 %all-to-all-start = ((bf16[24,8,1152]{2,1,0:T(8,128)(2,1)}), bf16[24,8,1152]{2,1,0:T(8,128)(2,1)S(1)}, u32[]{:S(2)}, u32[]{:S(2)}) async-start(bf16[24,8,1152]{2,1,0:T(8,128)(2,1)} %broadcast_in_dim.42), calls=%async_computation | async-start | bytes 884736 | tf_op jit(solution)/shard_map/all_to_all | solution.py:53
  23.2 14.7 %all-to-all-done = bf16[24,8,1152]{2,1,0:T(8,128)(2,1)S(1)} async-done(((bf16[24,8,1152]{2,1,0:T(8,128)(2,1)}), bf16[24,8,1152]{2,1,0:T(8,128)(2,1)S(1)}, u32[]{:S(2)}, u32[]{:S(2)}) %all-to-all-start) | async-done | bytes 442400 | tf_op jit(solution)/shard_map/all_to_all | solution.py:53
  38.0 2.4 %all_gather.17 = bf16[2,192,1152]{2,1,0:T(8,128)(2,1)S(1)} all-gather(bf16[1,192,1152]{2,1,0:T(8,128)(2,1)S(1)} %bitcast.21), channel_id=1, replica_groups=mesh['x'=4,'yh'=4,'z'=12,'yl'=2,'c'=2] {'c'}, dimensions={0}, use_global_device_ids=true | all-gather | bytes 1327104 | tf_op jit(solution)/shard_map/all_gather | solution.py:80
  40.4 0.5 fusion.8
  40.9 0.1 mul.176
  41.0 0.5 fusion.1
  41.5 0.1 select_convert_fusion
  41.6 0.1 pad_maximum_fusion
  41.8 26.4 %all_to_all.10 = f16[24,8,1280]{2,1,0:T(8,128)(2,1)S(1)} all-to-all(f16[24,8,1280]{2,1,0:T(8,128)(2,1)S(1)} %pad_maximum_fusion), channel_id=1, replica_groups={{0,4,8,2,6,10,48,52,56,50,54,58,96,100,104,98,102,106,144,148,152,146,1..., dimensions={0} | all-to-all | bytes 983040 | tf_op jit(solution)/shard_map/all_to_all | solution.py:53
  68.1 0.1 convert_reduce_fusion
  68.2 0.2 multiply_reduce_fusion
  68.4 0.1 fusion.24
  68.5 0.1 subtract_multiply_fusion
  68.5 0.1 fusion.16
  68.6 1.9 %all-gather.1 = f32[16,1280]{1,0:T(8,128)S(1)} all-gather(f32[8,1280]{1,0:T(8,128)S(1)} %pad_maximum_fusion.1), channel_id=3, replica_groups=mesh['x'=4,'yh'=4,'z'=12,'yl'=2,'c'=2] {'c'}, dimensions={0}, use_global_device_ids=true | all-gather | bytes 122880 | tf_op jit(solution)/shard_map/all_gather | solution.py:114
  70.5 0.6 deal_rows.1
  (12 shorter events, 0.1 us)
Async XLA Ops:
  0.7 0.7 copy-start.1
  0.7 0.7 copy-start
  14.5 23.4 %all-to-all-start = ((bf16[24,8,1152]{2,1,0:T(8,128)(2,1)}), bf16[24,8,1152]{2,1,0:T(8,128)(2,1)S(1)}, u32[]{:S(2)}, u32[]{:S(2)}) async-start(bf16[24,8,1152]{2,1,0:T(8,128)(2,1)} %broadcast_in_dim.42), calls=%async_computation | async-start | bytes 884736 | tf_op jit(solution)/shard_map/all_to_all | solution.py:53

commit v6 on v5

--- a/solution.py
+++ b/solution.py
@@ -12,14 +12,6 @@
 RUN = 3
 GAIN = 16.0
 LOSS_COLUMNS = 128
-
-
-def device_place(device):
-    coordinates = []
-    for size in reversed(SIZES):
-        coordinates.append(device % size)
-        device = device // size
-    return coordinates[::-1]
 
 
 def places(x, y, z):
@@ -66,47 +58,10 @@
     unit = values * inverse
     low = unit.astype(jnp.bfloat16)
     count = len(exchange_groups()[0])
-    pieces = jnp.broadcast_to(low[None], (count, chip_rows, width))
-    half_columns = jnp.int32(LOSS_COLUMNS // 2)
-    tied = lax.optimization_barrier((pieces, device, log_scale, bias, half_columns))
-    own, device, log_scale, bias, half_columns = lax.optimization_barrier(
-        (exchange(tied[0]),) + tied[1:]
-    )
-    scale_value = jnp.exp(log_scale[0])
-    bias_value = bias[0]
-    x, yh, z, yl, c = device_place(device)
-    own_is_text = c == 0
-    own = own.reshape(-1, width)
-    both = lax.all_gather(own, "c", axis=0)
-    other = jnp.where(own_is_text, both[1], both[0])
-    step, _, text_place, image_place = places(x, yh * SIZES[3] + yl, z)
-    has_twin = step == 0
-
-    def row_ids(place, axis):
-        return lax.broadcasted_iota(jnp.int32, (own.shape[0], own.shape[0]), axis) - chip_rows * place
-
-    def same_rows(text, image):
-        own_ids = row_ids(jnp.where(own_is_text, text, image), 0)
-        other_ids = row_ids(jnp.where(own_is_text, image, text), 1)
-        return (own_ids == other_ids) & (own_ids >= 0) & (own_ids < chip_rows)
-
-    positive = same_rows(text_place, image_place) | (
-        has_twin & same_rows(text_place + 1, image_place + 1)
-    )
-    counted = jnp.where(step == 1, 0.0, 1.0)
-    raw_logits = lax.dot_general(
-        own, other, (((1,), (1,)), ((), ())), preferred_element_type=jnp.float32
-    )
-    logits = scale_value * raw_logits + bias_value
-    labels = jnp.where(positive, 1.0, -1.0).astype(jnp.float32)
-    losses = counted * jnp.sum(jax.nn.softplus(-labels * logits), axis=1, keepdims=True)
-    coefs = (-scale_value * counted * labels * jax.nn.sigmoid(-labels * logits)).astype(jnp.bfloat16)
-    part = jnp.dot(coefs, other, preferred_element_type=jnp.float32) * GAIN
-    losses = losses * GAIN
-    rest = losses - losses.astype(jnp.float16).astype(jnp.float32)
-    upper = jnp.arange(LOSS_COLUMNS, dtype=jnp.int32)[None, :] >= half_columns
-    packed = jnp.concatenate([part, jnp.where(upper, rest, losses)], axis=1).astype(jnp.float16)
-    arrived = exchange(packed.reshape(count, chip_rows, -1))
+    own = exchange(jnp.broadcast_to(low[None], (count, chip_rows, width)))
+    both = lax.all_gather(own.reshape(-1, width), "c", axis=0)
+    packed = pair_block(both, log_scale, bias, count).astype(jnp.float16)
+    arrived = exchange(packed)
     total = jnp.sum(arrived.astype(jnp.float32), axis=0) * (1.0 / GAIN)
     upstream = total[:, :width]
     row_loss = (total[:, width:] + jnp.roll(total[:, width:], LOSS_COLUMNS // 2, axis=1)) / batch
@@ -114,6 +69,50 @@
     chip_grads = lax.all_gather(jnp.concatenate([grad, row_loss], axis=1), "c", axis=0)
     row_loss, image_grad, text_grad = deal_rows(chip_grads, rows, width)
     return (row_loss.reshape(rows), image_grad, text_grad)
+
+
+def block_kernel(both_ref, log_scale_ref, bias_ref, packed_ref):
+    count, chip_rows, _ = packed_ref.shape
+    width = both_ref.shape[2]
+    x, yh, z, yl, c = [lax.axis_index(name) for name in AXES]
+    own, other = both_ref[c], both_ref[1 - c]
+    step, _, text_place, image_place = places(x, yh * SIZES[3] + yl, z)
+    own_place = jnp.where(c == 0, text_place, image_place)
+    other_place = jnp.where(c == 0, image_place, text_place)
+    pairs = (own.shape[0], other.shape[0])
+    own_ids = lax.broadcasted_iota(jnp.int32, pairs, 0) - chip_rows * own_place
+    other_ids = lax.broadcasted_iota(jnp.int32, pairs, 1) - chip_rows * other_place
+    chips = jnp.where(step == 0, 2, 1)
+    positive = (own_ids == other_ids) & (own_ids >= 0) & (own_ids < chips * chip_rows)
+    counted = jnp.where(step == 1, 0.0, 1.0)
+    raw_logits = lax.dot_general(
+        own, other, (((1,), (1,)), ((), ())), preferred_element_type=jnp.float32
+    )
+    scale_value = jnp.exp(log_scale_ref[...])
+    logits = scale_value * raw_logits + bias_ref[...]
+    labels = jnp.where(positive, 1.0, -1.0)
+    margins = -labels * logits
+    softplus = jnp.maximum(margins, 0.0) + jnp.log1p(jnp.exp(-jnp.abs(margins)))
+    losses = (GAIN * counted) * jnp.sum(softplus, axis=1, keepdims=True)
+    coefs = ((-counted * scale_value) * labels * jax.nn.sigmoid(margins)).astype(jnp.bfloat16)
+    part = jnp.dot(coefs, other, preferred_element_type=jnp.float32) * GAIN
+    packed_ref[:, :, :width] = part.reshape(count, chip_rows, width)
+    rounded = losses.astype(jnp.bfloat16).astype(jnp.float32)
+    column = lax.broadcasted_iota(jnp.int32, (pairs[0], LOSS_COLUMNS), 1)
+    columns = jnp.where(column < LOSS_COLUMNS // 2, rounded, losses - rounded)
+    packed_ref[:, :, width:] = columns.reshape(count, chip_rows, LOSS_COLUMNS)
+
+
+def pair_block(both, log_scale, bias, count):
+    _, own_rows, width = both.shape
+    return pl.pallas_call(
+        block_kernel,
+        in_specs=[pl.BlockSpec(memory_space=pltpu.VMEM)] * 3,
+        out_specs=pl.BlockSpec(memory_space=pltpu.VMEM),
+        out_shape=jax.ShapeDtypeStruct((count, own_rows // count, width + LOSS_COLUMNS), jnp.float32),
+        compiler_params=pltpu.CompilerParams(vmem_limit_bytes=12 << 20),
+        name="pair_block",
+    )(both, log_scale.reshape(1, 1), bias.reshape(1, 1))
 
 
 def deal_kernel(chip_ref, loss_ref, image_ref, text_ref):

time: 71.5 us -> 70.9 us (level)
  matrix products: 0.98 us -> 0 us
  Pallas kernels: 0.62 us -> 1.44 us
    dot_general x2 -> x0, matrix products: 0.98 us -> none  [the longest x1 0.5 us: on_device(): lax.dot_general(own, other, (((1,), (1,)), ((), ())), preferred_element_t...]
    pallas_call x0 -> x1, Pallas kernels: none -> 0.82 us  [pair_block(): pl.pallas_call(block_kernel, in_specs=[pl.BlockSpec(memory_space=pltpu.VM...]
where the time goes in v6:
time: 70.9 us; the launch traced here: 70.6 us
  blocking collectives  42.6 us (60%)
  waiting for transfers between devices  14.8 us (21%)
  starting transfers between devices  7.37 us (10%)
  between operations  2.02 us (3%)
  local copies, waits for them, and re-layouts  1.66 us (2%)
  Pallas kernels  1.44 us (2%)
    all_to_all x1, blocking collectives, exchange(): lax.all_to_all(pieces, AXES, 0, 0, axis_index_groups=exchange_groups(), t...  26.4 us
    all_to_all x1, waiting for transfers between devices, exchange(): lax.all_to_all(pieces, AXES, 0, 0, axis_index_groups=exchange_groups(), t...  14.8 us
    all_gather x1, blocking collectives, on_device(): lax.all_gather(jnp.concatenate([text_embeds, image_embeds], axis=0), 'c',...  12 us
    all_to_all x1, starting transfers between devices, exchange(): lax.all_to_all(pieces, AXES, 0, 0, axis_index_groups=exchange_groups(), t...  7.37 us
    all_gather x1, blocking collectives, on_device(): both = lax.all_gather(own.reshape(-1, width), 'c', axis=0)  2.43 us
    all_gather x1, blocking collectives, on_device(): lax.all_gather(jnp.concatenate([grad, row_loss], axis=1), 'c', axis=0)  1.85 us
  transfers between devices with their start and end apart: 1, of which 1 were waited for; matrix products, arithmetic and copies ran while one was open for 0% of the time, Pallas kernels for 0%

profile of v6, /device:TPU:1, one launch (start us, length us, event | category | flops | bytes accessed | tf_op | source)
XLA Modules:
  0.0 70.6 jit_solution(3030814238538826076)
XLA Ops:
  0.7 0.0 copy-start.1
  0.7 0.0 copy-start
  0.7 0.7 copy-done.1
  1.4 0.0 copy-done
  1.4 12.0 %all-gather = bf16[16,1152]{1,0:T(8,128)(2,1)S(1)} all-gather(bf16[8,1152]{1,0:T(8,128)(2,1)S(1)} %pad_maximum_fusion.1), channel_id=2, replica_groups=mesh['x'=4,'yh'=4,'z'=12,'yl'=2,'c'=2] {'c'}, dimensions={0}, use_global_device_ids=true | all-gather | bytes 55296 | tf_op jit(solution)/shard_map/all_gather | solution.py:54
  13.4 0.1 multiply_reduce_fusion.1
  13.5 0.1 rsqrt.12
  13.6 0.1 multiply_convert_fusion
  13.7 0.8 %broadcast_in_dim.2 = bf16[24,8,1152]{2,1,0:T(8,128)(2,1)} broadcast(bf16[8,1152]{1,0:T(8,128)(2,1)S(1)} %multiply_convert_fusion), dimensions={1,2} | broadcast | bytes 460800 | tf_op jit(solution)/shard_map/broadcast_in_dim | solution.py:61
  14.5 7.4 %all-to-all-start = ((bf16[24,8,1152]{2,1,0:T(8,128)(2,1)}), bf16[24,8,1152]{2,1,0:T(8,128)(2,1)S(1)}, u32[]{:S(2)}, u32[]{:S(2)}) async-start(bf16[24,8,1152]{2,1,0:T(8,128)(2,1)} %broadcast_in_dim.2), calls=%async_computation | async-start | bytes 884736 | tf_op jit(solution)/shard_map/all_to_all | solution.py:45
  23.2 14.8 %all-to-all-done = bf16[24,8,1152]{2,1,0:T(8,128)(2,1)S(1)} async-done(((bf16[24,8,1152]{2,1,0:T(8,128)(2,1)}), bf16[24,8,1152]{2,1,0:T(8,128)(2,1)S(1)}, u32[]{:S(2)}, u32[]{:S(2)}) %all-to-all-start) | async-done | bytes 442400 | tf_op jit(solution)/shard_map/all_to_all | solution.py:45
  37.9 2.4 %all_gather.17.both_ref = bf16[2,192,1152]{2,1,0:T(8,128)(2,1)S(1)} all-gather(bf16[1,192,1152]{2,1,0:T(8,128)(2,1)S(1)} %bitcast.9), channel_id=1, replica_groups=mesh['x'=4,'yh'=4,'z'=12,'yl'=2,'c'=2] {'c'}, dimensions={0}, use_global_device_ids=true | all-gather | bytes 1327104 | tf_op jit(solution)/shard_map/all_gather | solution.py:62
  40.4 0.8 %pair_block.1 = f32[24,8,1280]{2,1,0:T(8,128)S(1)} custom-call(bf16[2,192,1152]{2,1,0:T(8,128)(2,1)S(1)} %all_gather.17.both_ref, f32[1,1]{1,0:T(1,128)} %bitcast.6.log_scale_ref, f32[1,1]{1,0:T(1,128)} %bitcast.7.bias_ref), custom_call_target="tpu_custom_call" | custom-call | tf_op jit(solution)/shard_map/pair_block/pallas_call | solution.py:108
  41.2 0.1 convert_element_type.30
  41.2 26.4 %all_to_all.10 = f16[24,8,1280]{2,1,0:T(8,128)(2,1)S(1)} all-to-all(f16[24,8,1280]{2,1,0:T(8,128)(2,1)S(1)} %convert_element_type.30), channel_id=1, replica_groups={{0,4,8,2,6,10,48,52,56,50,54,58,96,100,104,98,102,106,144,148,152,146,1..., dimensions={0} | all-to-all | bytes 983040 | tf_op jit(solution)/shard_map/all_to_all | solution.py:45
  67.6 0.1 convert_reduce_fusion
  67.7 0.2 multiply_reduce_fusion
  67.9 0.1 fusion.3
  67.9 0.1 subtract_multiply_fusion
  68.0 0.1 fusion.1
  68.1 1.9 %all-gather.1 = f32[16,1280]{1,0:T(8,128)S(1)} all-gather(f32[8,1280]{1,0:T(8,128)S(1)} %pad_maximum_fusion), channel_id=3, replica_groups=mesh['x'=4,'yh'=4,'z'=12,'yl'=2,'c'=2] {'c'}, dimensions={0}, use_global_device_ids=true | all-gather | bytes 122880 | tf_op jit(solution)/shard_map/all_gather | solution.py:69
  70.0 0.6 deal_rows.1
  (5 shorter events, 0.1 us)
Async XLA Ops:
  0.7 0.7 copy-start.1
  0.7 0.7 copy-start
  14.5 23.4 %all-to-all-start = ((bf16[24,8,1152]{2,1,0:T(8,128)(2,1)}), bf16[24,8,1152]{2,1,0:T(8,128)(2,1)S(1)}, u32[]{:S(2)}, u32[]{:S(2)}) async-start(bf16[24,8,1152]{2,1,0:T(8,128)(2,1)} %broadcast_in_dim.2), calls=%async_computation | async-start | bytes 884736 | tf_op jit(solution)/shard_map/all_to_all | solution.py:45

commit v7 on v6

--- a/solution.py
+++ b/solution.py
@@ -1,3 +1,5 @@
+import functools
+
 import jax
 import jax.numpy as jnp
 from jax import lax
@@ -48,27 +50,73 @@
 def on_device(image_embeds, text_embeds, log_scale, bias):
     rows, width = image_embeds.shape
     batch = rows * lax.axis_size(AXES)
-    device = lax.axis_index(AXES)
-    is_text = device % SIZES[-1] == 0
     chip_rows = 2 * rows
     chip_embeds = lax.all_gather(jnp.concatenate([text_embeds, image_embeds], axis=0), "c", axis=0)
-    embeds = jnp.where(is_text, chip_embeds[:, :rows], chip_embeds[:, rows:]).reshape(chip_rows, width)
-    values = embeds.astype(jnp.float32)
+    count = len(exchange_groups()[0])
+    pieces, unit, inverse = unit_pieces(chip_embeds, count)
+    own = exchange(pieces)
+    both = lax.all_gather(own.reshape(-1, width), "c", axis=0)
+    packed = pair_block(both, log_scale, bias, count).astype(jnp.float16)
+    arrived = exchange(packed)
+    total = jnp.sum(arrived.astype(jnp.float32), axis=0)
+    chip_grads = lax.all_gather(chip_results(total, unit, inverse, batch), "c", axis=0)
+    row_loss, image_grad, text_grad = deal_rows(chip_grads, rows, width)
+    return (row_loss.reshape(rows), image_grad, text_grad)
+
+
+def unit_kernel(chip_ref, pieces_ref, unit_ref, inverse_ref):
+    count, chip_rows, _ = pieces_ref.shape
+    rows = chip_rows // 2
+    first, second = chip_ref[0].astype(jnp.float32), chip_ref[1].astype(jnp.float32)
+    upper = lax.broadcasted_iota(jnp.int32, first.shape, 0) < rows
+    text = jnp.where(upper, first, pltpu.roll(second, rows, 0))
+    images = jnp.where(upper, pltpu.roll(first, rows, 0), second)
+    values = jnp.where(lax.axis_index("c") == 0, text, images)
     inverse = lax.rsqrt(jnp.sum(values * values, axis=1, keepdims=True) + epsilon)
     unit = values * inverse
     low = unit.astype(jnp.bfloat16)
-    count = len(exchange_groups()[0])
-    own = exchange(jnp.broadcast_to(low[None], (count, chip_rows, width)))
-    both = lax.all_gather(own.reshape(-1, width), "c", axis=0)
-    packed = pair_block(both, log_scale, bias, count).astype(jnp.float16)
-    arrived = exchange(packed)
-    total = jnp.sum(arrived.astype(jnp.float32), axis=0) * (1.0 / GAIN)
-    upstream = total[:, :width]
-    row_loss = (total[:, width:] + jnp.roll(total[:, width:], LOSS_COLUMNS // 2, axis=1)) / batch
-    grad = inverse * (upstream - unit * jnp.sum(unit * upstream, axis=1, keepdims=True))
-    chip_grads = lax.all_gather(jnp.concatenate([grad, row_loss], axis=1), "c", axis=0)
-    row_loss, image_grad, text_grad = deal_rows(chip_grads, rows, width)
-    return (row_loss.reshape(rows), image_grad, text_grad)
+    for k in range(count):
+        pieces_ref[k] = low
+    unit_ref[...] = unit
+    inverse_ref[...] = jnp.broadcast_to(inverse, unit.shape)
+
+
+def unit_pieces(chip_embeds, count):
+    _, chip_rows, width = chip_embeds.shape
+    return pl.pallas_call(
+        unit_kernel,
+        in_specs=[pl.BlockSpec(memory_space=pltpu.VMEM)],
+        out_specs=[pl.BlockSpec(memory_space=pltpu.VMEM)] * 3,
+        out_shape=[
+            jax.ShapeDtypeStruct((count, chip_rows, width), jnp.bfloat16),
+            jax.ShapeDtypeStruct((chip_rows, width), jnp.float32),
+            jax.ShapeDtypeStruct((chip_rows, width), jnp.float32),
+        ],
+        compiler_params=pltpu.CompilerParams(vmem_limit_bytes=4 << 20),
+        name="unit_pieces",
+    )(chip_embeds)
+
+
+def results_kernel(batch, total_ref, unit_ref, inverse_ref, results_ref):
+    width = unit_ref.shape[1]
+    upstream = total_ref[:, :width] * (1.0 / GAIN)
+    unit = unit_ref[...]
+    along = jnp.sum(unit * upstream, axis=1, keepdims=True)
+    results_ref[:, :width] = inverse_ref[...] * (upstream - unit * along)
+    terms = total_ref[:, width:]
+    both = terms + pltpu.roll(terms, LOSS_COLUMNS // 2, 1)
+    results_ref[:, width:] = both * (1.0 / (GAIN * batch))
+
+
+def chip_results(total, unit, inverse, batch):
+    return pl.pallas_call(
+        functools.partial(results_kernel, batch),
+        in_specs=[pl.BlockSpec(memory_space=pltpu.VMEM)] * 3,
+        out_specs=pl.BlockSpec(memory_space=pltpu.VMEM),
+        out_shape=jax.ShapeDtypeStruct(total.shape, jnp.float32),
+        compiler_params=pltpu.CompilerParams(vmem_limit_bytes=2 << 20),
+        name="chip_results",
+    )(total, unit, inverse)
 
 
 def block_kernel(both_ref, log_scale_ref, bias_ref, packed_ref):

time: 70.9 us -> 70.4 us (level)
  local copies, waits for them, and re-layouts: 1.66 us -> 0 us
  Pallas kernels: 1.44 us -> 2.43 us
    pallas_call x0 -> x2, Pallas kernels: none -> 0.98 us  [the longest x1 0.9 us: unit_pieces(): pl.pallas_call(unit_kernel, in_specs=[pl.BlockSpec(memory_space=pltpu.VME...]
    broadcast_in_dim x1 -> x0, local copies, waits for them, and re-layouts: 0.81 us -> none  [on_device(): own = exchange(jnp.broadcast_to(low[None], (count, chip_rows, width)))]
    concatenate x1, other arithmetic: 0.01 us -> 0.73 us  [on_device(): jnp.concatenate([text_embeds, image_embeds], axis=0)]
where the time goes in v7:
time: 70.4 us; the launch traced here: 70 us
  blocking collectives  42.7 us (61%)
  waiting for transfers between devices  14.8 us (21%)
  starting transfers between devices  7.37 us (10%)
  Pallas kernels  2.43 us (3%)
  between operations  1.95 us (3%)
  other arithmetic  0.86 us (1%)
    all_to_all x1, blocking collectives, exchange(): lax.all_to_all(pieces, AXES, 0, 0, axis_index_groups=exchange_groups(), t...  26.4 us
    all_to_all x1, waiting for transfers between devices, exchange(): lax.all_to_all(pieces, AXES, 0, 0, axis_index_groups=exchange_groups(), t...  14.8 us
    all_gather x1, blocking collectives, on_device(): lax.all_gather(jnp.concatenate([text_embeds, image_embeds], axis=0), 'c',...  12 us
    all_to_all x1, starting transfers between devices, exchange(): lax.all_to_all(pieces, AXES, 0, 0, axis_index_groups=exchange_groups(), t...  7.37 us
    all_gather x1, blocking collectives, on_device(): both = lax.all_gather(own.reshape(-1, width), 'c', axis=0)  2.43 us
    all_gather x1, blocking collectives, on_device(): lax.all_gather(chip_results(total, unit, inverse, batch), 'c', axis=0)  1.86 us
  transfers between devices with their start and end apart: 1, of which 1 were waited for; matrix products, arithmetic and copies ran while one was open for 0% of the time, Pallas kernels for 0%

profile of v7, /device:TPU:1, one launch (start us, length us, event | category | flops | bytes accessed | tf_op | source)
XLA Modules:
  0.0 70.0 jit_solution(2200098915459054862)
XLA Ops:
  0.6 0.7 %pad_maximum_fusion = bf16[8,1152]{1,0:T(8,128)(2,1)S(1)} fusion(bf16[4,1152]{1,0:T(4,128)(2,1)} %param.4, bf16[4,1152]{1,0:T(4,128)(2,1)} %param.5), kind=kLoop, calls=%fused_computation.1 | loop fusion | flops 36864 | bytes 36864 | tf_op jit(solution)/shard_map/concatenate | solution.py:54
  1.4 12.0 %all-gather = bf16[16,1152]{1,0:T(8,128)(2,1)S(1)} all-gather(bf16[8,1152]{1,0:T(8,128)(2,1)S(1)} %pad_maximum_fusion), channel_id=2, replica_groups=mesh['x'=4,'yh'=4,'z'=12,'yl'=2,'c'=2] {'c'}, dimensions={0}, use_global_device_ids=true | all-gather | bytes 55296 | tf_op jit(solution)/shard_map/all_gather | solution.py:54
  13.4 0.9 %unit_pieces.1 = (bf16[24,8,1152]{2,1,0:T(8,128)(2,1)}, f32[8,1152]{1,0:T(8,128)S(1)}, f32[8,1152]{1,0:T(8,128)S(1)}) custom-call(bf16[2,8,1152]{2,1,0:T(8,128)(2,1)S(1)} %bitcast.9), custom_call_target="tpu_custom_call" | custom-call | tf_op jit(solution)/shard_map/unit_pieces/pallas_call | solution.py:86
  14.3 7.4 %all-to-all-start = ((bf16[24,8,1152]{2,1,0:T(8,128)(2,1)}), bf16[24,8,1152]{2,1,0:T(8,128)(2,1)S(1)}, u32[]{:S(2)}, u32[]{:S(2)}) async-start(bf16[24,8,1152]{2,1,0:T(8,128)(2,1)} %get-tuple-element.9), calls=%async_computation | async-start | bytes 884736 | tf_op jit(solution)/shard_map/all_to_all | solution.py:47
  22.9 14.8 %all-to-all-done = bf16[24,8,1152]{2,1,0:T(8,128)(2,1)S(1)} async-done(((bf16[24,8,1152]{2,1,0:T(8,128)(2,1)}), bf16[24,8,1152]{2,1,0:T(8,128)(2,1)S(1)}, u32[]{:S(2)}, u32[]{:S(2)}) %all-to-all-start) | async-done | bytes 442400 | tf_op jit(solution)/shard_map/all_to_all | solution.py:47
  37.7 2.4 %all_gather.17.both_ref = bf16[2,192,1152]{2,1,0:T(8,128)(2,1)S(1)} all-gather(bf16[1,192,1152]{2,1,0:T(8,128)(2,1)S(1)} %bitcast.10), channel_id=1, replica_groups=mesh['x'=4,'yh'=4,'z'=12,'yl'=2,'c'=2] {'c'}, dimensions={0}, use_global_device_ids=true | all-gather | bytes 1327104 | tf_op jit(solution)/shard_map/all_gather | solution.py:58
  40.1 0.8 %pair_block.1 = f32[24,8,1280]{2,1,0:T(8,128)S(1)} custom-call(bf16[2,192,1152]{2,1,0:T(8,128)(2,1)S(1)} %all_gather.17.both_ref, f32[1,1]{1,0:T(1,128)} %bitcast.6.log_scale_ref, f32[1,1]{1,0:T(1,128)} %bitcast.7.bias_ref), custom_call_target="tpu_custom_call" | custom-call | tf_op jit(solution)/shard_map/pair_block/pallas_call | solution.py:156
  41.0 0.1 convert_element_type.6
  41.0 26.4 %all_to_all.10 = f16[24,8,1280]{2,1,0:T(8,128)(2,1)S(1)} all-to-all(f16[24,8,1280]{2,1,0:T(8,128)(2,1)S(1)} %convert_element_type.6), channel_id=1, replica_groups={{0,4,8,2,6,10,48,52,56,50,54,58,96,100,104,98,102,106,144,148,152,146,1..., dimensions={0} | all-to-all | bytes 983040 | tf_op jit(solution)/shard_map/all_to_all | solution.py:47
  67.4 0.1 convert_reduce_fusion.total_ref
  67.4 0.1 chip_results.1
  67.5 1.9 %all-gather.1 = f32[16,1280]{1,0:T(8,128)S(1)} all-gather(f32[8,1280]{1,0:T(8,128)S(1)} %chip_results.1), channel_id=3, replica_groups=mesh['x'=4,'yh'=4,'z'=12,'yl'=2,'c'=2] {'c'}, dimensions={0}, use_global_device_ids=true | all-gather | bytes 122880 | tf_op jit(solution)/shard_map/all_gather | solution.py:62
  69.4 0.6 deal_rows.1
Async XLA Ops:
  14.3 23.4 %all-to-all-start = ((bf16[24,8,1152]{2,1,0:T(8,128)(2,1)}), bf16[24,8,1152]{2,1,0:T(8,128)(2,1)S(1)}, u32[]{:S(2)}, u32[]{:S(2)}) async-start(bf16[24,8,1152]{2,1,0:T(8,128)(2,1)} %get-tuple-element.9), calls=%async_computation | async-start | bytes 884736 | tf_op jit(solution)/shard_map/all_to_all | solution.py:47

commit v8 on v7

--- a/solution.py
+++ b/solution.py
@@ -12,17 +12,19 @@
 AXES = ("x", "yh", "z", "yl", "c")
 SIZES = (4, 4, 12, 2, 2)
 RUN = 3
+TURN = 5
 GAIN = 16.0
 LOSS_COLUMNS = 128
 
 
 def places(x, y, z):
-    run, step = z // RUN, z % RUN
+    turned = (z + TURN) % SIZES[2]
+    run, step = turned // RUN, turned % RUN
     last, late = step // 2, run // 2
     half = (last + late) % 2
     text_place = RUN * y + step
     rank = last * (run + 2 * late) + (1 - last) * (2 * run - 2 * late + step)
-    return (step, half, text_place, 6 * x + rank)
+    return (run, step, half, text_place, 6 * x + rank)
 
 
 def exchange_groups():
@@ -34,8 +36,8 @@
             for z in range(zs):
                 for yl in range(yls):
                     y = yh * yls + yl
-                    _, half, text_place, image_place = places(x, y, z)
-                    text_key = (0, x, z // RUN)
+                    run, _, half, text_place, image_place = places(x, y, z)
+                    text_key = (0, x, run)
                     image_key = (1, y, half)
                     for core, key, place in ((0, text_key, text_place), (1, image_key, image_place)):
                         members.setdefault(key, []).append((place, device + core))
@@ -124,7 +126,7 @@
     width = both_ref.shape[2]
     x, yh, z, yl, c = [lax.axis_index(name) for name in AXES]
     own, other = both_ref[c], both_ref[1 - c]
-    step, _, text_place, image_place = places(x, yh * SIZES[3] + yl, z)
+    _, step, _, text_place, image_place = places(x, yh * SIZES[3] + yl, z)
     own_place = jnp.where(c == 0, text_place, image_place)
     other_place = jnp.where(c == 0, image_place, text_place)
     pairs = (own.shape[0], other.shape[0])

time: 70.4 us -> 67.6 us (0.960)
  waiting for transfers between devices: 14.8 us -> 13.3 us
  blocking collectives: 42.7 us -> 41.4 us
    all_to_all x1, blocking collectives: 26.4 us -> 22.9 us  [exchange(): lax.all_to_all(pieces, AXES, 0, 0, axis_index_groups=exchange_groups(), t...]
    all_gather x1, blocking collectives: 2.43 us -> 4.61 us  [on_device(): both = lax.all_gather(own.reshape(-1, width), 'c', axis=0)]
    all_to_all x1, waiting for transfers between devices: 14.8 us -> 13.3 us  [exchange(): lax.all_to_all(pieces, AXES, 0, 0, axis_index_groups=exchange_groups(), t...]
where the time goes in v8:
time: 67.6 us; the launch traced here: 67.3 us
  blocking collectives  41.4 us (61%)
  waiting for transfers between devices  13.3 us (20%)
  starting transfers between devices  7.45 us (11%)
  Pallas kernels  2.43 us (4%)
  between operations  1.95 us (3%)
  other arithmetic  0.86 us (1%)
    all_to_all x1, blocking collectives, exchange(): lax.all_to_all(pieces, AXES, 0, 0, axis_index_groups=exchange_groups(), t...  22.9 us
    all_to_all x1, waiting for transfers between devices, exchange(): lax.all_to_all(pieces, AXES, 0, 0, axis_index_groups=exchange_groups(), t...  13.3 us
    all_gather x1, blocking collectives, on_device(): lax.all_gather(jnp.concatenate([text_embeds, image_embeds], axis=0), 'c',...  12 us
    all_to_all x1, starting transfers between devices, exchange(): lax.all_to_all(pieces, AXES, 0, 0, axis_index_groups=exchange_groups(), t...  7.45 us
    all_gather x1, blocking collectives, on_device(): both = lax.all_gather(own.reshape(-1, width), 'c', axis=0)  4.61 us
    all_gather x1, blocking collectives, on_device(): lax.all_gather(chip_results(total, unit, inverse, batch), 'c', axis=0)  1.86 us
  transfers between devices with their start and end apart: 1, of which 1 were waited for; matrix products, arithmetic and copies ran while one was open for 0% of the time, Pallas kernels for 0%

profile of v8, /device:TPU:1, one launch (start us, length us, event | category | flops | bytes accessed | tf_op | source)
XLA Modules:
  0.0 67.3 jit_solution(16668501684739133611)
XLA Ops:
  0.6 0.7 %pad_maximum_fusion = bf16[8,1152]{1,0:T(8,128)(2,1)S(1)} fusion(bf16[4,1152]{1,0:T(4,128)(2,1)} %param.4, bf16[4,1152]{1,0:T(4,128)(2,1)} %param.5), kind=kLoop, calls=%fused_computation.1 | loop fusion | flops 36864 | bytes 36864 | tf_op jit(solution)/shard_map/concatenate | solution.py:56
  1.4 12.0 %all-gather = bf16[16,1152]{1,0:T(8,128)(2,1)S(1)} all-gather(bf16[8,1152]{1,0:T(8,128)(2,1)S(1)} %pad_maximum_fusion), channel_id=2, replica_groups=mesh['x'=4,'yh'=4,'z'=12,'yl'=2,'c'=2] {'c'}, dimensions={0}, use_global_device_ids=true | all-gather | bytes 55296 | tf_op jit(solution)/shard_map/all_gather | solution.py:56
  13.4 0.9 %unit_pieces.1 = (bf16[24,8,1152]{2,1,0:T(8,128)(2,1)}, f32[8,1152]{1,0:T(8,128)S(1)}, f32[8,1152]{1,0:T(8,128)S(1)}) custom-call(bf16[2,8,1152]{2,1,0:T(8,128)(2,1)S(1)} %bitcast.9), custom_call_target="tpu_custom_call" | custom-call | tf_op jit(solution)/shard_map/unit_pieces/pallas_call | solution.py:88
  14.3 7.5 %all-to-all-start = ((bf16[24,8,1152]{2,1,0:T(8,128)(2,1)}), bf16[24,8,1152]{2,1,0:T(8,128)(2,1)S(1)}, u32[]{:S(2)}, u32[]{:S(2)}) async-start(bf16[24,8,1152]{2,1,0:T(8,128)(2,1)} %get-tuple-element.9), calls=%async_computation | async-start | bytes 884736 | tf_op jit(solution)/shard_map/all_to_all | solution.py:49
  23.0 13.3 %all-to-all-done = bf16[24,8,1152]{2,1,0:T(8,128)(2,1)S(1)} async-done(((bf16[24,8,1152]{2,1,0:T(8,128)(2,1)}), bf16[24,8,1152]{2,1,0:T(8,128)(2,1)S(1)}, u32[]{:S(2)}, u32[]{:S(2)}) %all-to-all-start) | async-done | bytes 442400 | tf_op jit(solution)/shard_map/all_to_all | solution.py:49
  36.3 4.6 %all_gather.17.both_ref = bf16[2,192,1152]{2,1,0:T(8,128)(2,1)S(1)} all-gather(bf16[1,192,1152]{2,1,0:T(8,128)(2,1)S(1)} %bitcast.10), channel_id=1, replica_groups=mesh['x'=4,'yh'=4,'z'=12,'yl'=2,'c'=2] {'c'}, dimensions={0}, use_global_device_ids=true | all-gather | bytes 1327104 | tf_op jit(solution)/shard_map/all_gather | solution.py:60
  40.9 0.8 %pair_block.1 = f32[24,8,1280]{2,1,0:T(8,128)S(1)} custom-call(bf16[2,192,1152]{2,1,0:T(8,128)(2,1)S(1)} %all_gather.17.both_ref, f32[1,1]{1,0:T(1,128)} %bitcast.6.log_scale_ref, f32[1,1]{1,0:T(1,128)} %bitcast.7.bias_ref), custom_call_target="tpu_custom_call" | custom-call | tf_op jit(solution)/shard_map/pair_block/pallas_call | solution.py:158
  41.7 0.1 convert_element_type.6
  41.8 22.9 %all_to_all.10 = f16[24,8,1280]{2,1,0:T(8,128)(2,1)S(1)} all-to-all(f16[24,8,1280]{2,1,0:T(8,128)(2,1)S(1)} %convert_element_type.6), channel_id=1, replica_groups={{28,32,36,30,34,38,76,80,84,78,82,86,124,128,132,126,130,134,172,176,18..., dimensions={0} | all-to-all | bytes 983040 | tf_op jit(solution)/shard_map/all_to_all | solution.py:49
  64.7 0.1 convert_reduce_fusion.total_ref
  64.7 0.1 chip_results.1
  64.8 1.9 %all-gather.1 = f32[16,1280]{1,0:T(8,128)S(1)} all-gather(f32[8,1280]{1,0:T(8,128)S(1)} %chip_results.1), channel_id=3, replica_groups=mesh['x'=4,'yh'=4,'z'=12,'yl'=2,'c'=2] {'c'}, dimensions={0}, use_global_device_ids=true | all-gather | bytes 122880 | tf_op jit(solution)/shard_map/all_gather | solution.py:64
  66.7 0.6 deal_rows.1
Async XLA Ops:
  14.3 22.0 %all-to-all-start = ((bf16[24,8,1152]{2,1,0:T(8,128)(2,1)}), bf16[24,8,1152]{2,1,0:T(8,128)(2,1)S(1)}, u32[]{:S(2)}, u32[]{:S(2)}) async-start(bf16[24,8,1152]{2,1,0:T(8,128)(2,1)} %get-tuple-element.9), calls=%async_computation | async-start | bytes 884736 | tf_op jit(solution)/shard_map/all_to_all | solution.py:49

commit v9 on v8

--- a/solution.py
+++ b/solution.py
@@ -12,7 +12,7 @@
 AXES = ("x", "yh", "z", "yl", "c")
 SIZES = (4, 4, 12, 2, 2)
 RUN = 3
-TURN = 5
+TURN = 3
 GAIN = 16.0
 LOSS_COLUMNS = 128
 

time: 67.6 us -> 65.9 us (0.975)
  waiting for transfers between devices: 13.3 us -> 9.97 us
  starting transfers between devices: 7.45 us -> 8.36 us
    all_to_all x1, waiting for transfers between devices: 13.3 us -> 9.97 us  [exchange(): lax.all_to_all(pieces, AXES, 0, 0, axis_index_groups=exchange_groups(), t...]
    all_to_all x1, blocking collectives: 22.9 us -> 25.6 us  [exchange(): lax.all_to_all(pieces, AXES, 0, 0, axis_index_groups=exchange_groups(), t...]
    all_gather x1, blocking collectives: 4.61 us -> 2.43 us  [on_device(): both = lax.all_gather(own.reshape(-1, width), 'c', axis=0)]
    all_to_all x1, starting transfers between devices: 7.45 us -> 8.36 us  [exchange(): lax.all_to_all(pieces, AXES, 0, 0, axis_index_groups=exchange_groups(), t...]
where the time goes in v9:
time: 65.9 us; the launch traced here: 65.6 us
  blocking collectives  42 us (64%)
  waiting for transfers between devices  9.97 us (15%)
  starting transfers between devices  8.36 us (13%)
  Pallas kernels  2.43 us (4%)
  between operations  1.95 us (3%)
  other arithmetic  0.86 us (1%)
    all_to_all x1, blocking collectives, exchange(): lax.all_to_all(pieces, AXES, 0, 0, axis_index_groups=exchange_groups(), t...  25.6 us
    all_gather x1, blocking collectives, on_device(): lax.all_gather(jnp.concatenate([text_embeds, image_embeds], axis=0), 'c',...  12 us
    all_to_all x1, waiting for transfers between devices, exchange(): lax.all_to_all(pieces, AXES, 0, 0, axis_index_groups=exchange_groups(), t...  9.97 us
    all_to_all x1, starting transfers between devices, exchange(): lax.all_to_all(pieces, AXES, 0, 0, axis_index_groups=exchange_groups(), t...  8.36 us
    all_gather x1, blocking collectives, on_device(): both = lax.all_gather(own.reshape(-1, width), 'c', axis=0)  2.43 us
    all_gather x1, blocking collectives, on_device(): lax.all_gather(chip_results(total, unit, inverse, batch), 'c', axis=0)  1.93 us
  transfers between devices with their start and end apart: 1, of which 1 were waited for; matrix products, arithmetic and copies ran while one was open for 0% of the time, Pallas kernels for 0%

profile of v9, /device:TPU:1, one launch (start us, length us, event | category | flops | bytes accessed | tf_op | source)
XLA Modules:
  0.0 65.6 jit_solution(5086380384683598491)
XLA Ops:
  0.6 0.7 %pad_maximum_fusion = bf16[8,1152]{1,0:T(8,128)(2,1)S(1)} fusion(bf16[4,1152]{1,0:T(4,128)(2,1)} %param.4, bf16[4,1152]{1,0:T(4,128)(2,1)} %param.5), kind=kLoop, calls=%fused_computation.1 | loop fusion | flops 36864 | bytes 36864 | tf_op jit(solution)/shard_map/concatenate | solution.py:56
  1.4 12.0 %all-gather = bf16[16,1152]{1,0:T(8,128)(2,1)S(1)} all-gather(bf16[8,1152]{1,0:T(8,128)(2,1)S(1)} %pad_maximum_fusion), channel_id=2, replica_groups=mesh['x'=4,'yh'=4,'z'=12,'yl'=2,'c'=2] {'c'}, dimensions={0}, use_global_device_ids=true | all-gather | bytes 55296 | tf_op jit(solution)/shard_map/all_gather | solution.py:56
  13.4 0.9 %unit_pieces.1 = (bf16[24,8,1152]{2,1,0:T(8,128)(2,1)}, f32[8,1152]{1,0:T(8,128)S(1)}, f32[8,1152]{1,0:T(8,128)S(1)}) custom-call(bf16[2,8,1152]{2,1,0:T(8,128)(2,1)S(1)} %bitcast.9), custom_call_target="tpu_custom_call" | custom-call | tf_op jit(solution)/shard_map/unit_pieces/pallas_call | solution.py:88
  14.3 8.4 %all-to-all-start = ((bf16[24,8,1152]{2,1,0:T(8,128)(2,1)}), bf16[24,8,1152]{2,1,0:T(8,128)(2,1)S(1)}, u32[]{:S(2)}, u32[]{:S(2)}) async-start(bf16[24,8,1152]{2,1,0:T(8,128)(2,1)} %get-tuple-element.9), calls=%async_computation | async-start | bytes 884736 | tf_op jit(solution)/shard_map/all_to_all | solution.py:49
  23.9 10.0 %all-to-all-done = bf16[24,8,1152]{2,1,0:T(8,128)(2,1)S(1)} async-done(((bf16[24,8,1152]{2,1,0:T(8,128)(2,1)}), bf16[24,8,1152]{2,1,0:T(8,128)(2,1)S(1)}, u32[]{:S(2)}, u32[]{:S(2)}) %all-to-all-start) | async-done | bytes 442400 | tf_op jit(solution)/shard_map/all_to_all | solution.py:49
  33.9 2.4 %all_gather.17.both_ref = bf16[2,192,1152]{2,1,0:T(8,128)(2,1)S(1)} all-gather(bf16[1,192,1152]{2,1,0:T(8,128)(2,1)S(1)} %bitcast.10), channel_id=1, replica_groups=mesh['x'=4,'yh'=4,'z'=12,'yl'=2,'c'=2] {'c'}, dimensions={0}, use_global_device_ids=true | all-gather | bytes 1327104 | tf_op jit(solution)/shard_map/all_gather | solution.py:60
  36.3 0.8 %pair_block.1 = f32[24,8,1280]{2,1,0:T(8,128)S(1)} custom-call(bf16[2,192,1152]{2,1,0:T(8,128)(2,1)S(1)} %all_gather.17.both_ref, f32[1,1]{1,0:T(1,128)} %bitcast.6.log_scale_ref, f32[1,1]{1,0:T(1,128)} %bitcast.7.bias_ref), custom_call_target="tpu_custom_call" | custom-call | tf_op jit(solution)/shard_map/pair_block/pallas_call | solution.py:158
  37.2 0.1 convert_element_type.6
  37.2 25.6 %all_to_all.10 = f16[24,8,1280]{2,1,0:T(8,128)(2,1)S(1)} all-to-all(f16[24,8,1280]{2,1,0:T(8,128)(2,1)S(1)} %convert_element_type.6), channel_id=1, replica_groups={{36,40,44,38,42,46,84,88,92,86,90,94,132,136,140,134,138,142,180,184,18..., dimensions={0} | all-to-all | bytes 983040 | tf_op jit(solution)/shard_map/all_to_all | solution.py:49
  62.8 0.1 convert_reduce_fusion.total_ref
  62.9 0.1 chip_results.1
  63.0 1.9 %all-gather.1 = f32[16,1280]{1,0:T(8,128)S(1)} all-gather(f32[8,1280]{1,0:T(8,128)S(1)} %chip_results.1), channel_id=3, replica_groups=mesh['x'=4,'yh'=4,'z'=12,'yl'=2,'c'=2] {'c'}, dimensions={0}, use_global_device_ids=true | all-gather | bytes 122880 | tf_op jit(solution)/shard_map/all_gather | solution.py:64
  64.9 0.6 deal_rows.1
Async XLA Ops:
  14.3 19.6 %all-to-all-start = ((bf16[24,8,1152]{2,1,0:T(8,128)(2,1)}), bf16[24,8,1152]{2,1,0:T(8,128)(2,1)S(1)}, u32[]{:S(2)}, u32[]{:S(2)}) async-start(bf16[24,8,1152]{2,1,0:T(8,128)(2,1)} %get-tuple-element.9), calls=%async_computation | async-start | bytes 884736 | tf_op jit(solution)/shard_map/all_to_all | solution.py:49

commit v10 on v9

--- a/solution.py
+++ b/solution.py
@@ -22,7 +22,7 @@
     run, step = turned // RUN, turned % RUN
     last, late = step // 2, run // 2
     half = (last + late) % 2
-    text_place = RUN * y + step
+    text_place = RUN * ((y + 4) % 8) + step
     rank = last * (run + 2 * late) + (1 - last) * (2 * run - 2 * late + step)
     return (run, step, half, text_place, 6 * x + rank)
 

time: 65.9 us -> 65.1 us (0.988)
  waiting for transfers between devices: 9.97 us -> 8.46 us
  blocking collectives: 42 us -> 42.7 us
    all_to_all x1, waiting for transfers between devices: 9.97 us -> 8.46 us  [exchange(): lax.all_to_all(pieces, AXES, 0, 0, axis_index_groups=exchange_groups(), t...]
    all_to_all x1, blocking collectives: 25.6 us -> 26.4 us  [exchange(): lax.all_to_all(pieces, AXES, 0, 0, axis_index_groups=exchange_groups(), t...]
where the time goes in v10:
time: 65.1 us; the launch traced here: 64.8 us
  blocking collectives  42.7 us (66%)
  waiting for transfers between devices  8.46 us (13%)
  starting transfers between devices  8.36 us (13%)
  Pallas kernels  2.43 us (4%)
  between operations  1.95 us (3%)
  other arithmetic  0.86 us (1%)
    all_to_all x1, blocking collectives, exchange(): lax.all_to_all(pieces, AXES, 0, 0, axis_index_groups=exchange_groups(), t...  26.4 us
    all_gather x1, blocking collectives, on_device(): lax.all_gather(jnp.concatenate([text_embeds, image_embeds], axis=0), 'c',...  12 us
    all_to_all x1, waiting for transfers between devices, exchange(): lax.all_to_all(pieces, AXES, 0, 0, axis_index_groups=exchange_groups(), t...  8.46 us
    all_to_all x1, starting transfers between devices, exchange(): lax.all_to_all(pieces, AXES, 0, 0, axis_index_groups=exchange_groups(), t...  8.36 us
    all_gather x1, blocking collectives, on_device(): both = lax.all_gather(own.reshape(-1, width), 'c', axis=0)  2.43 us
    all_gather x1, blocking collectives, on_device(): lax.all_gather(chip_results(total, unit, inverse, batch), 'c', axis=0)  1.86 us
  transfers between devices with their start and end apart: 1, of which 1 were waited for; matrix products, arithmetic and copies ran while one was open for 0% of the time, Pallas kernels for 0%

profile of v10, /device:TPU:1, one launch (start us, length us, event | category | flops | bytes accessed | tf_op | source)
XLA Modules:
  0.0 64.8 jit_solution(16999117580229002760)
XLA Ops:
  0.6 0.7 %pad_maximum_fusion = bf16[8,1152]{1,0:T(8,128)(2,1)S(1)} fusion(bf16[4,1152]{1,0:T(4,128)(2,1)} %param.4, bf16[4,1152]{1,0:T(4,128)(2,1)} %param.5), kind=kLoop, calls=%fused_computation.1 | loop fusion | flops 36864 | bytes 36864 | tf_op jit(solution)/shard_map/concatenate | solution.py:56
  1.4 12.0 %all-gather = bf16[16,1152]{1,0:T(8,128)(2,1)S(1)} all-gather(bf16[8,1152]{1,0:T(8,128)(2,1)S(1)} %pad_maximum_fusion), channel_id=2, replica_groups=mesh['x'=4,'yh'=4,'z'=12,'yl'=2,'c'=2] {'c'}, dimensions={0}, use_global_device_ids=true | all-gather | bytes 55296 | tf_op jit(solution)/shard_map/all_gather | solution.py:56
  13.4 0.9 %unit_pieces.1 = (bf16[24,8,1152]{2,1,0:T(8,128)(2,1)}, f32[8,1152]{1,0:T(8,128)S(1)}, f32[8,1152]{1,0:T(8,128)S(1)}) custom-call(bf16[2,8,1152]{2,1,0:T(8,128)(2,1)S(1)} %bitcast.9), custom_call_target="tpu_custom_call" | custom-call | tf_op jit(solution)/shard_map/unit_pieces/pallas_call | solution.py:88
  14.3 8.4 %all-to-all-start = ((bf16[24,8,1152]{2,1,0:T(8,128)(2,1)}), bf16[24,8,1152]{2,1,0:T(8,128)(2,1)S(1)}, u32[]{:S(2)}, u32[]{:S(2)}) async-start(bf16[24,8,1152]{2,1,0:T(8,128)(2,1)} %get-tuple-element.9), calls=%async_computation | async-start | bytes 884736 | tf_op jit(solution)/shard_map/all_to_all | solution.py:49
  23.9 8.5 %all-to-all-done = bf16[24,8,1152]{2,1,0:T(8,128)(2,1)S(1)} async-done(((bf16[24,8,1152]{2,1,0:T(8,128)(2,1)}), bf16[24,8,1152]{2,1,0:T(8,128)(2,1)S(1)}, u32[]{:S(2)}, u32[]{:S(2)}) %all-to-all-start) | async-done | bytes 442400 | tf_op jit(solution)/shard_map/all_to_all | solution.py:49
  32.4 2.4 %all_gather.17.both_ref = bf16[2,192,1152]{2,1,0:T(8,128)(2,1)S(1)} all-gather(bf16[1,192,1152]{2,1,0:T(8,128)(2,1)S(1)} %bitcast.10), channel_id=1, replica_groups=mesh['x'=4,'yh'=4,'z'=12,'yl'=2,'c'=2] {'c'}, dimensions={0}, use_global_device_ids=true | all-gather | bytes 1327104 | tf_op jit(solution)/shard_map/all_gather | solution.py:60
  34.8 0.8 %pair_block.1 = f32[24,8,1280]{2,1,0:T(8,128)S(1)} custom-call(bf16[2,192,1152]{2,1,0:T(8,128)(2,1)S(1)} %all_gather.17.both_ref, f32[1,1]{1,0:T(1,128)} %bitcast.6.log_scale_ref, f32[1,1]{1,0:T(1,128)} %bitcast.7.bias_ref), custom_call_target="tpu_custom_call" | custom-call | tf_op jit(solution)/shard_map/pair_block/pallas_call | solution.py:158
  35.6 0.1 convert_element_type.6
  35.7 26.4 %all_to_all.10 = f16[24,8,1280]{2,1,0:T(8,128)(2,1)S(1)} all-to-all(f16[24,8,1280]{2,1,0:T(8,128)(2,1)S(1)} %convert_element_type.6), channel_id=1, replica_groups={{132,136,140,134,138,142,180,184,188,182,186,190,36,40,44,38,42,46,84,8..., dimensions={0} | all-to-all | bytes 983040 | tf_op jit(solution)/shard_map/all_to_all | solution.py:49
  62.1 0.1 convert_reduce_fusion.total_ref
  62.2 0.1 chip_results.1
  62.3 1.9 %all-gather.1 = f32[16,1280]{1,0:T(8,128)S(1)} all-gather(f32[8,1280]{1,0:T(8,128)S(1)} %chip_results.1), channel_id=3, replica_groups=mesh['x'=4,'yh'=4,'z'=12,'yl'=2,'c'=2] {'c'}, dimensions={0}, use_global_device_ids=true | all-gather | bytes 122880 | tf_op jit(solution)/shard_map/all_gather | solution.py:64
  64.1 0.6 deal_rows.1
Async XLA Ops:
  14.3 18.1 %all-to-all-start = ((bf16[24,8,1152]{2,1,0:T(8,128)(2,1)}), bf16[24,8,1152]{2,1,0:T(8,128)(2,1)S(1)}, u32[]{:S(2)}, u32[]{:S(2)}) async-start(bf16[24,8,1152]{2,1,0:T(8,128)(2,1)} %get-tuple-element.9), calls=%async_computation | async-start | bytes 884736 | tf_op jit(solution)/shard_map/all_to_all | solution.py:49
